TPU v7x, 128 devices: a whole 4x4x4 slice. The times are simulated.
128 devices in a mesh: ctx: 32 (over y_lo, z, x), fsdp: 4 (over y_hi, core).
Axes of the slice: x: 4, y: 4 (y_hi: 2, y_lo: 2; y = y_hi * 2 + y_lo), z: 4, core: 2. Of those that a mesh axis runs over, the one named last changes fastest.
Arguments:
- inputs: bfloat16 [4, 4096, 4096], P('fsdp', 'ctx'), may hold values from -6 to 6
- values: bfloat16 [4, 4096, 8192], P('fsdp', 'ctx'), may hold values from -6 to 6
- cotangent: bfloat16 [4, 4096, 8192], P('fsdp', 'ctx'), may hold values from -6 to 6
- weight: bfloat16 [4096, 1152], P('fsdp'), may hold values from -0.0234375 to 0.0234375
- init_state: bfloat16 [4, 128, 4096], P('fsdp'), may hold values from -1.1953125 to 1.1953125
- resets: int32 [4, 4096], P('fsdp', 'ctx'), may hold values from 0 to 1, as said below
- dt_bias: float32 [128], replicated, may hold values from -5 to -3
- decay_rate: float32 [128], replicated, may hold values from 9.765625e-05 to 1.5
- skip: float32 [128], replicated, may hold values from 0.5 to 1.5
Outputs:
- grad_inputs: bfloat16 [4, 4096, 4096], P('fsdp', 'ctx')
- grad_values: bfloat16 [4, 4096, 8192], P('fsdp', 'ctx')
- grad_weight: float32 [4096, 1152], P('fsdp')
Inputs may be any that keep to these rules, and one draw needn't show every extreme that they name: `resets`: each stream flags one or two of its positions.
All inputs are finite; a program needn't handle non-finite values.
Results may differ from a plain program's by a relative error of at most 0.015.
Values may be sent and summed in bfloat16 or wider, within the bound.
A program may use at most 256 MiB of HBM per device.

v0:
```python
import math

import jax
import jax.numpy as jnp
from jax import lax
from jax.sharding import PartitionSpec as P

HEAD_DIM = 64
STATE = 64
GROUPS = 8


def prefix(part, axis, combine, identity, reverse):
    count = lax.axis_size(axis)
    place = lax.axis_index(axis)
    ahead = count - 1 - place if reverse else place
    gathered = jax.tree.map(lambda a: lax.all_gather(a, axis), part)
    state = jax.tree.map(lambda a, e: jnp.zeros_like(a) + jnp.asarray(e, a.dtype), part, identity)

    def one(lap, state):
        source = count - 1 - lap if reverse else lap
        return combine(
            state, jax.tree.map(lambda a: lax.dynamic_index_in_dim(a, source, 0, False), gathered)
        )

    return lax.fori_loop(0, ahead, one, state)


def prepare(raw_step, value_rows, dt_bias):
    step_size = jax.nn.softplus(raw_step + dt_bias[None, :])
    discrete = (step_size[:, :, None] * value_rows.astype(jnp.float32)).astype(jnp.bfloat16)
    return (step_size, discrete)


def block_stats(b_proj, step_size, discrete, decay_rate, segment):
    tokens, heads = step_size.shape
    per_group = heads // GROUPS
    log_decay = jnp.cumsum(-decay_rate[None, :] * step_size, axis=0)
    final = log_decay[-1]
    same = segment == segment[-1]
    tail = jnp.where(same[:, None], jnp.exp(final[None, :] - log_decay), 0.0)
    total = jnp.where(segment[-1] == 0, jnp.exp(final), 0.0)
    weighted = (tail[:, :, None] * discrete.astype(jnp.float32)).astype(jnp.bfloat16)
    local = jnp.einsum(
        "sgkp,sgn->gkpn",
        weighted.reshape(tokens, GROUPS, per_group, HEAD_DIM),
        b_proj,
        preferred_element_type=jnp.float32,
    )
    return (total, local.reshape(heads, HEAD_DIM * STATE))


def group_terms(c_group, b_group, log_group, disc_group, state_group, valid, fresh):
    scores = jnp.einsum("tn,sn->ts", c_group, b_group, preferred_element_type=jnp.float32)
    spans = log_group.T[:, :, None] - log_group.T[:, None, :]
    weights = jnp.where(valid, jnp.exp(jnp.where(valid, spans, 0.0)), 0.0)
    mixed = (weights * scores[None, :, :]).astype(jnp.bfloat16)
    inner = jnp.einsum("kts,skp->tkp", mixed, disc_group, preferred_element_type=jnp.float32)
    carried = jnp.einsum(
        "tn,kpn->tkp", c_group.astype(jnp.float32), state_group, precision=lax.Precision.HIGHEST
    )
    reach = jnp.where(fresh[:, None], jnp.exp(log_group), 0.0)
    return inner + reach[:, :, None] * carried


def block_out(
    b_proj, c_proj, step_size, discrete, value_rows, start_state, decay_rate, skip, segment
):
    tokens, heads = step_size.shape
    per_group = heads // GROUPS
    log_decay = jnp.cumsum(-decay_rate[None, :] * step_size, axis=0)
    position = jnp.arange(tokens)
    valid = (position[None, :] <= position[:, None]) & (segment[:, None] == segment[None, :])
    fresh = segment == 0
    state_three = start_state.reshape(heads, HEAD_DIM, STATE)
    pieces = []
    for which in range(GROUPS):
        first_head = which * per_group
        last_head = first_head + per_group
        pieces.append(
            jax.checkpoint(group_terms)(
                c_proj[:, which],
                b_proj[:, which],
                log_decay[:, first_head:last_head],
                discrete[:, first_head:last_head],
                state_three[first_head:last_head],
                valid,
                fresh,
            )
        )
    return jnp.concatenate(pieces, axis=1) + skip[None, :, None] * value_rows.astype(jnp.float32)


def chain_forward(earlier, later):
    return (earlier[0] * later[0], later[0][:, None] * earlier[1] + later[1])


def chain_backward(earlier, later):
    return (earlier[0] * later[0], later[1] + later[0][:, None] * earlier[1])


def body(inputs, values, cotangent, weight, init_state, resets, dt_bias, decay_rate, skip):
    tokens = inputs.shape[1]
    heads = dt_bias.shape[0]
    width = GROUPS * STATE
    token_rows = inputs[0]
    full_weight = lax.all_gather(weight, "fsdp", axis=0, tiled=True)
    proj = jnp.dot(token_rows, full_weight, preferred_element_type=jnp.float32)
    b_proj = proj[:, :width].astype(jnp.bfloat16).reshape(tokens, GROUPS, STATE)
    c_proj = proj[:, width : 2 * width].astype(jnp.bfloat16).reshape(tokens, GROUPS, STATE)
    raw_step = proj[:, 2 * width :]
    value_rows = values[0].reshape(tokens, heads, HEAD_DIM)
    segment = jnp.cumsum(resets[0])
    (step_size, discrete), prep_pull = jax.vjp(
        lambda raw, vals: prepare(raw, vals, dt_bias), raw_step, value_rows
    )
    (total, local), stats_pull = jax.vjp(
        lambda bmat, steps, disc: block_stats(bmat, steps, disc, decay_rate, segment),
        b_proj,
        step_size,
        discrete,
    )
    neutral = (jnp.ones_like(total), jnp.zeros_like(local))
    before, arrived = prefix((total, local), "ctx", chain_forward, neutral, False)
    start_state = before[:, None] * init_state[0].astype(jnp.float32) + arrived

    def outputs(bmat, cmat, steps, disc, vals, state):
        return block_out(bmat, cmat, steps, disc, vals, state, decay_rate, skip, segment)

    _, out_pull = jax.vjp(outputs, b_proj, c_proj, step_size, discrete, value_rows, start_state)
    grad_heads = cotangent[0].reshape(tokens, heads, HEAD_DIM).astype(jnp.float32)
    d_b_out, d_c, d_step_out, d_disc_out, d_val_out, d_start = out_pull(grad_heads)
    _, end_grad = prefix((total, d_start), "ctx", chain_backward, neutral, True)
    d_total = jnp.sum(end_grad * start_state, axis=1)
    d_b_stats, d_step_stats, d_disc_stats = stats_pull((d_total, end_grad))
    d_b = d_b_out + d_b_stats
    d_disc = d_disc_out + d_disc_stats
    d_raw, d_val_prep = prep_pull((d_step_out + d_step_stats, d_disc))
    grad_vals = (d_val_out + d_val_prep).reshape(tokens, heads * HEAD_DIM)
    d_proj = jnp.concatenate(
        [d_b.reshape(tokens, width), d_c.reshape(tokens, width), d_raw.astype(jnp.bfloat16)], axis=1
    )
    grad_in = jnp.einsum("qc,dc->qd", d_proj, full_weight, preferred_element_type=jnp.float32)
    grad_in = grad_in.astype(jnp.bfloat16)
    ctx_count = lax.axis_size("ctx")
    fsdp_count = lax.axis_size("fsdp")
    scale = 1.0 / math.sqrt(fsdp_count * tokens * ctx_count)
    own_rows = lax.psum_scatter(
        jnp.einsum("qd,qc->dc", token_rows, d_proj, preferred_element_type=jnp.float32),
        "fsdp",
        scatter_dimension=0,
        tiled=True,
    )
    grad_w = lax.psum(own_rows, "ctx")
    return (grad_in[None], grad_vals[None], grad_w * scale)


def solution(mesh):
    in_specs = (
        P("fsdp", "ctx", None),
        P("fsdp", "ctx", None),
        P("fsdp", "ctx", None),
        P("fsdp", None),
        P("fsdp", None, None),
        P("fsdp", "ctx"),
        P(),
        P(),
        P(),
    )
    out_specs = (P("fsdp", "ctx", None), P("fsdp", "ctx", None), P("fsdp", None))
    return jax.shard_map(body, mesh=mesh, in_specs=in_specs, out_specs=out_specs, check_vma=False)
```

profile of v0, /device:TPU:0, one launch (start us, length us, event | category | flops | bytes accessed | tf_op | source)
XLA Modules:
  0.0 2280.9 jit_solution(5002639962010622302)
XLA Ops:
  9.6 2.9 copy.209
  13.7 66.8 %all-gather.5.cloned.1.call-done = bf16[4096,1152]{1,0:T(8,128)(2,1)} async-done(((bf16[1024,1152]{1,0:T(8,128)(2,1)}), bf16[4096,1152]{1,0:T(8,128)(2,1)}) %all-gather.5.cloned.1.call-update) | async-done | bytes 9437200 | tf_op jit(solution)/shard_map/all_gather | solution.py:107
  80.5 5.2 fusion.287
  87.1 2.8 multiply_convert_fusion.1
  91.3 2.7 fusion.11
  94.0 4.8 reshape.306
  100.4 2.9 copy.214
  104.0 4.2 fusion.282
  108.3 83.1 %all-gather = f32[32,1,128]{2,1,0:T(1,128)} all-gather(f32[1,1,128]{2,1,0:T(1,128)S(1)} %get-tuple-element.376), channel_id=1, replica_groups=mesh['ctx'=32,'fsdp'=4] {'ctx'}, dimensions={0}, use_global_device_ids=true | all-gather | bytes 16896 | tf_op jit(solution)/shard_map/all_gather | solution.py:17
  193.4 3.0 multiply_convert_fusion.2
  197.8 613.9 %all-gather.7.cloned.1.call-done = f32[32,128,4096]{2,1,0:T(8,128)} async-done(((f32[1,128,4096]{2,1,0:T(8,128)}), f32[32,128,4096]{2,1,0:T(8,128)}) %all-gather.7.cloned.1.call-update) | async-done | bytes 67108880 | tf_op jit(solution)/shard_map/all_gather | solution.py:17
  854.3 3.3 fusion.197
  857.7 3.4 fusion.194
  861.0 6.7 pad_add_fusion
  867.8 4.8 copy.222
  872.5 2.9 copy.223
  878.7 2.6 reduce_window_sum.40
  896.5 2.1 fusion.42
  916.7 755.1 %all-gather.9.cloned.1.call-done = f32[32,128,4096]{2,1,0:T(8,128)} async-done(((f32[1,128,4096]{2,1,0:T(8,128)}), f32[32,128,4096]{2,1,0:T(8,128)}) %all-gather.9.cloned.1.call-update) | async-done | bytes 67108880 | tf_op jit(solution)/shard_map/all_gather | solution.py:17
  1672.0 87.4 %while.27 = (s32[]{:T(128)}, f32[128,4096]{1,0:T(8,128)S(1)}, s32[]{:T(128)}, f32[32,128,4096]{2,1,0:T(8,128)}, f32[32,128]{1,0:T(8,128)}, /*index=5*/s32[]{:T(128)}, s32[]{:T(128)}, s32[]{:T(128)}, s32[]{:T(128)}) while((s32[]{:T(128)}, f32[128,4096]{1,0:T(8,128)S(1)}, s32[]{:T(128)}, f32[32,128,4096]{2,1,0:T(8,128)}, ...), condition=%wide.region_13.14_spmd, body=%wide.region_12.13_spmd.sunk | while | flops 1048582 | bytes 6293147 | solution.py:26
  1706.5 2.1 bitcast_add_fusion.21
  1761.3 3.0 reshape.308
  1764.4 5.0 fusion.2
  1770.7 7.1 fusion.6
  1782.7 2.5 fusion.38
  1785.2 8.5 convolution_bitcast_fusion
  1794.1 142.2 %reduce-scatter.2.cloned.1.call-done = f32[1024,1152]{0,1:T(8,128)} async-done(((f32[4096,1152]{0,1:T(8,128)}), f32[1024,1152]{0,1:T(8,128)}) %reduce-scatter.2.cloned.1.call-update) | async-done | bytes 4718608 | tf_op jit(solution)/shard_map/reduce_scatter | solution.py:148
  1937.9 2.9 copy.238
  1940.8 7.8 fusion
  1948.6 313.9 %all-reduce.43.cloned.1.call-done = f32[1024,1152]{0,1:T(8,128)} async-done(((f32[1024,1152]{0,1:T(8,128)}), f32[1024,1152]{0,1:T(8,128)}) %all-reduce.43.cloned.1.call-update) | async-done | bytes 4718608 | tf_op jit(solution)/shard_map/psum | solution.py:154
  2262.5 5.5 broadcast_multiply_fusion
  2268.0 6.0 copy.239
  (481 shorter events, 183.6 us)
Async XLA Ops:
  7.2 73.3 %copy-start = (bf16[1,128,4096]{2,1,0:T(8,128)(2,1)S(1)}, bf16[1,128,4096]{2,1,0:T(8,128)(2,1)}, u32[]{:S(2)}) copy-start(bf16[1,128,4096]{2,1,0:T(8,128)(2,1)} %param.13) | copy-start | bytes 3145732
  7.2 73.3 %all-gather.5.cloned.1.call-start = ((), (), s32[]{:S(2)}) async-start(), calls=%async_computation.1 | async-start | bytes 11796480 | tf_op jit(solution)/shard_map/all_gather | solution.py:107
  7.9 803.8 %all-gather.7.cloned.1.call-start = ((), (), s32[]{:S(2)}) async-start(), calls=%async_computation.2 | async-start | bytes 69206016 | tf_op jit(solution)/shard_map/all_gather | solution.py:17
  8.9 77.6 %copy-start.143 = (f32[128]{0:T(128)}, f32[128]{0:T(128)S(1)}, u32[]{:S(2)}) copy-start(f32[128]{0:T(128)S(1)} %neg.52) | copy-start | bytes 1540
  13.7 76.4 %copy-start.139 = (pred[128]{0:T(512)(128)(4,1)}, pred[128]{0:T(512)(128)(4,1)S(1)}, u32[]{:S(2)}) copy-start(pred[128]{0:T(512)(128)(4,1)S(1)} %get-tuple-element.394) | copy-start | bytes 388
  13.7 72.9 %copy-start.141 = (f32[128]{0:T(128)S(1)}, f32[128]{0:T(128)}, u32[]{:S(2)}) copy-start(f32[128]{0:T(128)} %param.19) | copy-start | bytes 1540
  98.8 1573.0 %all-gather.9.cloned.1.call-start = ((), (), s32[]{:S(2)}) async-start(), calls=%async_computation.3 | async-start | bytes 69206016 | tf_op jit(solution)/shard_map/all_gather | solution.py:17
  193.4 633.7 %copy-start.65 = (bf16[128,64]{0,1:T(8,128)(2,1)}, bf16[128,64]{0,1:T(8,128)(2,1)S(1)}, u32[]{:S(2)}) copy-start(bf16[128,64]{0,1:T(8,128)(2,1)S(1)} %get-tuple-element.249) | copy-start | bytes 49156
  193.4 639.0 %copy-start.77 = (bf16[128,64]{0,1:T(8,128)(2,1)}, bf16[128,64]{0,1:T(8,128)(2,1)S(1)}, u32[]{:S(2)}) copy-start(bf16[128,64]{0,1:T(8,128)(2,1)S(1)} %get-tuple-element.237) | copy-start | bytes 49156
  193.4 639.6 %copy-start.75 = (bf16[128,64]{0,1:T(8,128)(2,1)}, bf16[128,64]{0,1:T(8,128)(2,1)S(1)}, u32[]{:S(2)}) copy-start(bf16[128,64]{0,1:T(8,128)(2,1)S(1)} %get-tuple-element.239) | copy-start | bytes 49156
  193.4 648.0 %copy-start.71 = (bf16[128,64]{0,1:T(8,128)(2,1)}, bf16[128,64]{0,1:T(8,128)(2,1)S(1)}, u32[]{:S(2)}) copy-start(bf16[128,64]{0,1:T(8,128)(2,1)S(1)} %get-tuple-element.243) | copy-start | bytes 49156
  816.3 11.0 copy-start.20
  816.5 10.2 copy-start.18
  816.5 10.0 copy-start.41
  816.5 10.2 copy-start.15
  831.2 29.8 %copy-start.97 = (f32[128,16]{0,1:T(8,128)}, f32[128,16]{0,1:T(8,128)S(1)}, u32[]{:S(2)}) copy-start(f32[128,16]{0,1:T(8,128)S(1)} %get-tuple-element.399) | copy-start | bytes 24580
  875.5 1060.8 %reduce-scatter.2.cloned.1.call-start = ((), (), s32[]{:S(2)}) async-start(), calls=%async_computation.4 | async-start | bytes 23592960 | tf_op jit(solution)/shard_map/reduce_scatter | solution.py:148
  881.2 17.4 copy-start.76
  881.2 17.4 copy-start.80
  881.2 17.6 copy-start.29
  881.2 17.6 copy-start.92
  881.2 18.7 copy-start.74
  881.3 18.7 copy-start.82
  881.3 18.9 copy-start.10
  881.3 18.9 copy-start.27
  881.3 18.9 copy-start.90
  888.9 12.4 copy-start.72
  888.9 12.4 copy-start.81
  891.9 9.5 copy-start.12
  891.9 9.6 copy-start.25
  891.9 9.6 copy-start.96
  1793.8 468.8 %all-reduce.43.cloned.1.call-start = ((), (), s32[]{:S(2)}) async-start(), calls=%async_computation.5 | async-start | bytes 9437184 | tf_op jit(solution)/shard_map/psum | solution.py:154
  (121 other events, 426.9 us)
Sparse Core Ops, SparseCore 0:
  9.7 70.7 all-gather.4
  98.9 712.7 all-gather.6
  875.6 796.2 all-gather.8
  1793.9 142.3 reduce-scatter.1
  1938.8 323.6 all-reduce.42
where the time goes:
time: 2290 us; the launch traced here: 2280 us
  waiting for transfers between devices  1890 us (83%)
  matrix products  104 us (5%)
  other arithmetic  101 us (4%)
  blocking collectives  83.1 us (4%)
  local copies, waits for them, and re-layouts  81.6 us (4%)
    all_gather x2, waiting for transfers between devices, prefix(): gathered = jax.tree.map(lambda a: lax.all_gather(a, axis), part)  1370 us
    psum x1, waiting for transfers between devices, body(): grad_w = lax.psum(own_rows, 'ctx')  314 us
    reduce_scatter x1, waiting for transfers between devices, body(): lax.psum_scatter(jnp.einsum('qd,qc->dc', token_rows, d_proj, preferred_el...  142 us
    all_gather x1, blocking collectives, prefix(): gathered = jax.tree.map(lambda a: lax.all_gather(a, axis), part)  83.1 us
    all_gather x1, waiting for transfers between devices, body(): full_weight = lax.all_gather(weight, 'fsdp', axis=0, tiled=True)  66.8 us
    add x31, other arithmetic, chain_backward(): return (earlier[0] * later[0], later[1] + later[0][:, None] * earlier[1])  65.3 us
  transfers between devices with their start and end apart: 5, of which 5 were waited for; matrix products, arithmetic and copies ran while one was open for 3% of the time, Pallas kernels for 0%

commit v1 on v0

v1 whole, which is shorter than its diff:
```python
import functools
import math

import jax
import jax.numpy as jnp
from jax import lax
from jax.experimental import pallas as pl
from jax.experimental.pallas import tpu as pltpu
from jax.sharding import PartitionSpec as P

MESH = pl.DeviceIdType.MESH
F32 = jnp.float32
BF16 = jnp.bfloat16
TOK = 128
HEADS = 128
GROUPS = 8
STATE = 64
WIDE = 1024
COLS = 1152
MSG = 144
OWN = 256
VMEM = pl.BlockSpec(memory_space=pltpu.VMEM)


def nn(a, b):
    return lax.dot_general(a, b, (((1,), (0,)), ((), ())), preferred_element_type=F32)


def nt(a, b):
    return lax.dot_general(a, b, (((1,), (1,)), ((), ())), preferred_element_type=F32)


def tn(a, b):
    return lax.dot_general(a, b, (((0,), (0,)), ((), ())), preferred_element_type=F32)


def split2(x):
    high = x.astype(BF16)
    return high, (x - high.astype(F32)).astype(BF16)


def split3(x):
    high, rest = x.astype(BF16), None
    rest = x - high.astype(F32)
    mid = rest.astype(BF16)
    return high, mid, (rest - mid.astype(F32)).astype(BF16)


def exact(mat, x):
    return sum(nn(mat, part) for part in split3(x))


def remote(src, dst, ssem, rsem, to):
    return pltpu.make_async_remote_copy(
        src_ref=src, dst_ref=dst, send_sem=ssem, recv_sem=rsem, device_id=to, device_id_type=MESH
    )


def project_kernel(x_ref, w_ref, b_ref, c_ref, raw_ref, wsib_ref, xr_ref, xs_ref,
                   part_bc, part_raw, got_bc, got_raw, ssem, rsem):
    me, f = lax.axis_index("ctx"), lax.axis_index("fsdp")
    core = lax.rem(f, 2)
    chip = f // 2
    sib = (me, f + 1 - 2 * core)
    far = (me, lax.rem(f + 2, 4))
    bar = pltpu.get_barrier_semaphore()
    for to in (sib, far):
        pl.semaphore_signal(bar, inc=1, device_id=to, device_id_type=MESH)
    pl.semaphore_wait(bar, 2)
    send_x = remote(x_ref.at[:, pl.ds(pl.multiple_of((1 - chip) * 2048, 2048), 2048)], xr_ref,
                    ssem.at[0], rsem.at[0], far)
    send_x.start()
    send_w = remote(w_ref, wsib_ref, ssem.at[1], rsem.at[1], sib)
    send_w.start()
    mine = pl.multiple_of(core * 1024, 1024)
    other = pl.multiple_of((1 - core) * 1024, 1024)
    base = chip * 2048
    send_xo = remote(x_ref.at[:, pl.ds(pl.multiple_of(base + other, 1024), 1024)], xs_ref.at[0],
                     ssem.at[2], rsem.at[2], sib)
    send_xo.start()
    own = nn(x_ref[:, pl.ds(pl.multiple_of(base + mine, 1024), 1024)], w_ref[...])
    send_w.wait_recv()
    own += nn(x_ref[:, pl.ds(pl.multiple_of(base + other, 1024), 1024)], wsib_ref[...])
    send_x.wait_recv()
    send_xr = remote(xr_ref.at[:, pl.ds(other, 1024)], xs_ref.at[1], ssem.at[3], rsem.at[3], sib)
    send_xr.start()
    away = nn(xr_ref[:, pl.ds(mine, 1024)], w_ref[...]) + nn(xr_ref[:, pl.ds(other, 1024)], wsib_ref[...])
    part_bc[...] = away[:, :1024].astype(BF16)
    part_raw[...] = away[:, 1024:]
    send_bc = remote(part_bc, got_bc, ssem.at[4], rsem.at[4], far)
    send_bc.start()
    send_raw = remote(part_raw, got_raw, ssem.at[5], rsem.at[5], far)
    send_raw.start()
    send_bc.wait_recv()
    send_raw.wait_recv()
    full = (own[:, :1024] + got_bc[...].astype(F32)).astype(BF16)
    for g in range(GROUPS):
        b_ref[g] = full[:, g * STATE:(g + 1) * STATE]
        c_ref[g] = full[:, 512 + g * STATE:512 + (g + 1) * STATE]
    raw_ref[...] = own[:, 1024:] + got_raw[...]
    for one in (send_xo, send_xr):
        one.wait_recv()
    for one in (send_x, send_w, send_xo, send_xr, send_bc, send_raw):
        one.wait_send()


def project(x, w):
    shapes = (
        jax.ShapeDtypeStruct((GROUPS, TOK, STATE), BF16),
        jax.ShapeDtypeStruct((GROUPS, TOK, STATE), BF16),
        jax.ShapeDtypeStruct((TOK, HEADS), F32),
        jax.ShapeDtypeStruct((1024, COLS), BF16),
        jax.ShapeDtypeStruct((TOK, 2048), BF16),
        jax.ShapeDtypeStruct((2, TOK, 1024), BF16),
    )
    return pl.pallas_call(
        project_kernel,
        out_shape=shapes,
        in_specs=[VMEM] * 2,
        out_specs=[VMEM] * 6,
        scratch_shapes=[
            pltpu.VMEM((TOK, 1024), BF16),
            pltpu.VMEM((TOK, HEADS), F32),
            pltpu.VMEM((TOK, 1024), BF16),
            pltpu.VMEM((TOK, HEADS), F32),
            pltpu.SemaphoreType.DMA((6,)),
            pltpu.SemaphoreType.DMA((6,)),
        ],
        compiler_params=pltpu.CompilerParams(
            collective_id=0, has_side_effects=True, vmem_limit_bytes=48 * 2**20
        ),
        name="project",
    )(x, w)


def block_masks(resets_ref):
    flags = resets_ref[...].astype(F32)
    row = lax.broadcasted_iota(jnp.int32, (TOK, TOK), 0)
    col = lax.broadcasted_iota(jnp.int32, (TOK, TOK), 1)
    seg_col = jnp.sum(jnp.where(col <= row, flags, 0.0), axis=1, keepdims=True)
    flag_col = jnp.sum(jnp.where(col == row, flags, 0.0), axis=1, keepdims=True)
    seg_row = jnp.sum(jnp.where(row <= col, flag_col, 0.0), axis=0, keepdims=True)
    valid = (col <= row) & (seg_col == seg_row)
    return row, col, valid, seg_col


def spread_matrix(g):
    head = lax.rem(lax.broadcasted_iota(jnp.int32, (256, WIDE), 0), 128)
    lane = lax.broadcasted_iota(jnp.int32, (256, WIDE), 1) // STATE
    return jnp.where(head == lane + 16 * g, 1.0, 0.0).astype(BF16)


def gather_matrix(g):
    lane = lax.broadcasted_iota(jnp.int32, (WIDE, HEADS), 0) // STATE
    head = lax.broadcasted_iota(jnp.int32, (WIDE, HEADS), 1)
    return jnp.where(head == lane + 16 * g, 1.0, 0.0).astype(BF16)


def per_head(x, mat):
    high, low = split2(x)
    return nn(high, mat) + nn(low, mat)


def states_kernel(b_ref, c_ref, raw_ref, val_ref, cot_ref, resets_ref, bias_ref, rate_ref, skip_ref,
                  init_ref, dproj_ref, gval_ref,
                  disc_ref, wgt_ref, rc_ref, step_ref, skipx_ref, totx_ref, dd_ref, logt_ref, logd_ref,
                  dlog_ref, dstep_ref, db_ref, dc_ref, out_ref, in_ref, back_ref, home_ref,
                  s1, r1, s2, r2, lsem):
    n = lax.axis_size("ctx")
    me, f = lax.axis_index("ctx"), lax.axis_index("fsdp")
    my_row, my_x = me // 4, lax.rem(me, 4)
    bar = pltpu.get_barrier_semaphore()

    def greet(i, carry):
        pl.semaphore_signal(bar, inc=1, device_id=(lax.rem(me + i, n), f), device_id_type=MESH)
        return carry

    lax.fori_loop(1, n, greet, 0)
    row, col, valid, seg_col = block_masks(resets_ref)
    raw = raw_ref[...] + bias_ref[...]
    step = jnp.maximum(raw, 0.0) + jnp.log1p(jnp.exp(-jnp.abs(raw)))
    low_tri = jnp.where(col <= row, 1.0, 0.0).astype(BF16)
    log_decay = exact(low_tri, -rate_ref[...] * step)
    final = log_decay[TOK - 1:, :]
    last_seg = seg_col[TOK - 1:, :]
    tail = jnp.where(seg_col == last_seg, jnp.exp(final - log_decay), 0.0)
    reach = jnp.where(seg_col == 0.0, jnp.exp(log_decay), 0.0)
    total = jnp.where(last_seg == 0.0, jnp.exp(final), 0.0)
    logd_ref[...] = log_decay
    logt_ref[...] = jnp.transpose(log_decay)
    few = lax.broadcasted_iota(jnp.int32, (16, HEADS), 0)
    extra = jnp.where(few < 8, skip_ref[...], total)
    stack = jnp.concatenate([step, tail, reach, extra], axis=0)
    stack = jnp.concatenate(split2(stack), axis=1)
    pl.semaphore_wait(bar, n - 1)

    def wide(g):
        return pl.ds(pl.multiple_of(g * WIDE, WIDE), WIDE)

    def out_copy(to):
        return remote(out_ref.at[to], in_ref.at[me], s1.at[to], r1.at[me], (to, f))

    def own_copy():
        return pltpu.make_async_copy(out_ref.at[me], in_ref.at[me], lsem)

    def produce(i, carry):
        g = lax.rem(my_row + i, GROUPS)
        spread = nn(stack, spread_matrix(g))
        step_x = spread[:TOK]
        cot = cot_ref[:, wide(g)].astype(F32)
        disc = (step_x * val_ref[:, wide(g)].astype(F32)).astype(BF16)
        wgt = (spread[TOK:2 * TOK] * disc.astype(F32)).astype(BF16)
        rc = (spread[2 * TOK:3 * TOK] * cot).astype(BF16)
        step_ref[g] = step_x
        skipx_ref[g] = spread[3 * TOK:3 * TOK + 8]
        totx_ref[g] = spread[3 * TOK + 8:3 * TOK + 16]
        disc_ref[g] = disc
        wgt_ref[g] = wgt
        rc_ref[g] = rc
        local = tn(b_ref[g], wgt).astype(BF16)
        first = tn(c_ref[g], rc).astype(BF16)
        tot = spread[3 * TOK + 8:3 * TOK + 9]
        high, low = split2(tot)
        which = lax.broadcasted_iota(jnp.int32, (16, WIDE), 0)
        tots = jnp.where(which == 0, high.astype(F32), jnp.where(which == 1, low.astype(F32), 0.0)).astype(BF16)
        for j in range(4):
            to = g * 4 + j
            lanes = slice(j * OWN, (j + 1) * OWN)
            out_ref[to, :64, :] = local[:, lanes]
            out_ref[to, 64:128, :] = first[:, lanes]
            out_ref[to, 128:, :] = tots[:, lanes]
        for j in range(4):
            to = g * 4 + lax.rem(my_x + j, 4)

            @pl.when(to != me)
            def _():
                out_copy(to).start()

            @pl.when(to == me)
            def _():
                own_copy().start()

        return carry

    lax.fori_loop(0, GROUPS, produce, 0)

    dlog_ref[...] = jnp.zeros_like(dlog_ref)
    half = lax.broadcasted_iota(jnp.int32, (1, TOK), 1) < STATE
    left = jnp.where(half, 1.0, 0.0)
    left_b = left.astype(BF16)
    right_b = (1.0 - left).astype(BF16)
    bad = jnp.where(valid, 0.0, 1.0)

    def inside(g, carry):
        b, c = b_ref[g], c_ref[g]
        scores = nt(c, b)
        logs = pltpu.roll(logd_ref[...], lax.rem(HEADS - 16 * g, HEADS), 1)
        d_scores = jnp.zeros((TOK, TOK), F32)
        errs = []
        for q in range(8):
            lanes = pl.ds(pl.multiple_of(g * WIDE + q * 128, 128), 128)
            cot_p = cot_ref[:, lanes]
            disc_p = disc_ref[g, :, q * 128:(q + 1) * 128]
            stacked = jnp.concatenate([disc_p * left_b, disc_p * right_b], axis=0)
            d_mixed = nt(cot_p, stacked)
            mixed = []
            for k in range(2):
                head = 2 * q + k
                span = logs[:, head:head + 1] - logt_ref[pl.ds(g * 16 + head, 1), :]
                weights = jnp.exp(jnp.where(valid, span, -1e30))
                d_scores += d_mixed[:, k * TOK:(k + 1) * TOK] * weights
                mixed.append((weights * scores).astype(BF16))
            mixed = jnp.concatenate(mixed, axis=1)
            inner = nn(mixed, stacked)
            both = tn(mixed, cot_p)
            dd = both[:TOK] * left + both[TOK:] * (1.0 - left)
            dd_ref[g, :, q * 128:(q + 1) * 128] = dd.astype(BF16)
            errs.append(cot_p.astype(F32) * inner - disc_p.astype(F32) * dd)
        dlog_ref[...] += per_head(jnp.concatenate(errs, axis=1), gather_matrix(g))
        ds = d_scores.astype(BF16)
        dc_ref[g] = nn(ds, b)
        db_ref[g] = tn(ds, c)
        return carry

    lax.fori_loop(0, GROUPS, inside, 0)

    own_copy().wait()

    def arrive(i, carry):
        src = lax.rem(me + n - i, n)
        remote(out_ref.at[src], in_ref.at[src], s1.at[src], r1.at[src], (src, f)).wait_recv()
        return carry

    lax.fori_loop(1, n, arrive, 0)

    def lap_total(j):
        return jnp.sum(in_ref[j, 128:, :].astype(F32), axis=0, keepdims=True)

    def forward(j, state):
        back_ref[j, :64, :] = state.astype(BF16)
        return lap_total(j) * state + in_ref[j, :64, :].astype(F32)

    lax.fori_loop(0, n, forward, init_ref[...].astype(F32))

    def backward(i, state):
        j = n - 1 - i
        back_ref[j, 64:, :] = state.astype(BF16)
        return in_ref[j, 64:128, :].astype(F32) + lap_total(j) * state

    lax.fori_loop(0, n, backward, jnp.zeros((STATE, OWN), F32))

    def back_copy(to):
        return remote(back_ref.at[to], home_ref.at[me], s2.at[to], r2.at[me], (to, f))

    def own_back():
        return pltpu.make_async_copy(back_ref.at[me], home_ref.at[me], lsem)

    own_back().start()

    def send_back(i, carry):
        back_copy(lax.rem(me + i, n)).start()
        return carry

    lax.fori_loop(1, n, send_back, 0)
    own_back().wait()
    dstep_ref[...] = jnp.zeros_like(dstep_ref)

    def consume(i, carry):
        g = lax.rem(my_row + GROUPS - i, GROUPS)
        for j in range(4):
            src = g * 4 + j

            @pl.when(src != me)
            def _():
                remote(back_ref.at[src], home_ref.at[src], s2.at[src], r2.at[src], (src, f)).wait_recv()

        got = jnp.concatenate([home_ref[g * 4 + j] for j in range(4)], axis=1)
        start, end = got[:64], got[64:]
        b, c = b_ref[g], c_ref[g]
        rc, wgt, disc = rc_ref[g], wgt_ref[g], disc_ref[g].astype(F32)
        carried = nn(c, start)
        d_wgt = nn(b, end)
        dc_ref[g] += nt(rc, start)
        db_ref[g] += nt(wgt, end)
        pull = wgt.astype(F32) * d_wgt
        mat = gather_matrix(g)
        err = rc.astype(F32) * carried - pull
        ends = jnp.sum(pull, axis=0, keepdims=True)
        ends += totx_ref[g, :1, :] * jnp.sum(start.astype(F32) * end.astype(F32), axis=0, keepdims=True)
        at_end = lax.broadcasted_iota(jnp.int32, (TOK, WIDE), 0) == TOK - 1
        err = err + jnp.where(at_end, ends, 0.0)
        dlog_ref[...] += per_head(err, mat)
        spread = nn(stack[TOK:2 * TOK], spread_matrix(g))
        d_disc = dd_ref[g].astype(F32) + spread * d_wgt
        val = val_ref[:, wide(g)].astype(F32)
        dstep_ref[...] += per_head(d_disc * val, mat)
        gval = skipx_ref[g, :1, :] * cot_ref[:, wide(g)].astype(F32) + step_ref[g] * d_disc
        gval_ref[:, wide(g)] = gval.astype(BF16)
        return carry

    lax.fori_loop(0, GROUPS, consume, 0)
    up_tri = jnp.where(col >= row, 1.0, 0.0).astype(BF16)
    d_inc = exact(up_tri, dlog_ref[...])
    d_step = dstep_ref[...] - rate_ref[...] * d_inc
    d_raw = d_step / (1.0 + jnp.exp(-raw))
    pieces = [db_ref[g] for g in range(GROUPS)] + [dc_ref[g] for g in range(GROUPS)] + [d_raw]
    dproj_ref[...] = jnp.concatenate(pieces, axis=1).astype(BF16)

    def drain(i, carry):
        to = lax.rem(me + i, n)
        out_copy(to).wait_send()
        back_copy(to).wait_send()
        return carry

    lax.fori_loop(1, n, drain, 0)


def states(b, c, raw, val, cot, resets, bias, rate, skip, init):
    n = 32
    slab = (GROUPS, TOK, WIDE)
    return pl.pallas_call(
        states_kernel,
        out_shape=(
            jax.ShapeDtypeStruct((TOK, COLS), BF16),
            jax.ShapeDtypeStruct((TOK, GROUPS * WIDE), BF16),
        ),
        in_specs=[VMEM] * 10,
        out_specs=[VMEM] * 2,
        scratch_shapes=[
            pltpu.VMEM(slab, BF16),
            pltpu.VMEM(slab, BF16),
            pltpu.VMEM(slab, BF16),
            pltpu.VMEM(slab, F32),
            pltpu.VMEM((GROUPS, 8, WIDE), F32),
            pltpu.VMEM((GROUPS, 8, WIDE), F32),
            pltpu.VMEM(slab, BF16),
            pltpu.VMEM((HEADS, TOK), F32),
            pltpu.VMEM((TOK, HEADS), F32),
            pltpu.VMEM((TOK, HEADS), F32),
            pltpu.VMEM((TOK, HEADS), F32),
            pltpu.VMEM((GROUPS, TOK, STATE), F32),
            pltpu.VMEM((GROUPS, TOK, STATE), F32),
            pltpu.VMEM((n, MSG, OWN), BF16),
            pltpu.VMEM((n, MSG, OWN), BF16),
            pltpu.VMEM((n, 128, OWN), BF16),
            pltpu.VMEM((n, 128, OWN), BF16),
            pltpu.SemaphoreType.DMA((n,)),
            pltpu.SemaphoreType.DMA((n,)),
            pltpu.SemaphoreType.DMA((n,)),
            pltpu.SemaphoreType.DMA((n,)),
            pltpu.SemaphoreType.DMA,
        ],
        compiler_params=pltpu.CompilerParams(
            collective_id=1, has_side_effects=True, vmem_limit_bytes=56 * 2**20
        ),
        name="states",
    )(b, c, raw, val, cot, resets, bias, rate, skip, init)


def grads_kernel(scale, dp_ref, x_ref, xr_ref, xs_ref, w_ref, wsib_ref, gin_ref, gw_ref,
                 dps, away, gin_in, part, got, mine_b, full, ssem, rsem, s1, r1, s2, r2, lsem):
    n = lax.axis_size("ctx")
    me, f = lax.axis_index("ctx"), lax.axis_index("fsdp")
    core, chip = lax.rem(f, 2), f // 2
    sib = (me, f + 1 - 2 * core)
    far = (me, lax.rem(f + 2, 4))
    bar = pltpu.get_barrier_semaphore()
    for to in (sib, far):
        pl.semaphore_signal(bar, inc=1, device_id=to, device_id_type=MESH)

    def greet(i, carry):
        pl.semaphore_signal(bar, inc=1, device_id=(lax.rem(me + i, n), f), device_id_type=MESH)
        return carry

    lax.fori_loop(1, n, greet, 0)
    pl.semaphore_wait(bar, n + 1)
    send_far = remote(dp_ref, dps.at[0], ssem.at[0], rsem.at[0], far)
    send_far.start()
    send_sib = remote(dp_ref, dps.at[1], ssem.at[1], rsem.at[1], sib)
    send_sib.start()
    mine = pl.multiple_of(core * 1024, 1024)
    other = pl.multiple_of((1 - core) * 1024, 1024)
    base = chip * 2048
    own_at = pl.multiple_of(base + mine, 1024)
    other_at = pl.multiple_of(base + other, 1024)
    gin_ref[:, pl.ds(own_at, 1024)] = nt(dp_ref[...], w_ref[...]).astype(BF16)
    gin_ref[:, pl.ds(other_at, 1024)] = nt(dp_ref[...], wsib_ref[...]).astype(BF16)
    send_far.wait_recv()
    send_fwd = remote(dps.at[0], dps.at[2], ssem.at[2], rsem.at[2], sib)
    send_fwd.start()
    away[:, pl.ds(mine, 1024)] = nt(dps[0], w_ref[...]).astype(BF16)
    away[:, pl.ds(other, 1024)] = nt(dps[0], wsib_ref[...]).astype(BF16)
    send_gin = remote(away, gin_in, ssem.at[3], rsem.at[3], far)
    send_sib.wait_recv()
    send_fwd.wait_recv()
    xa = x_ref[:, pl.ds(own_at, 1024)]
    xb = xr_ref[:, pl.ds(mine, 1024)]
    xall = jnp.concatenate([xa, xb, xs_ref[0], xs_ref[1]], axis=0)
    dall = jnp.concatenate([dp_ref[...], dps[0], dps[1], dps[2]], axis=0)
    part[...] = tn(xall, dall).astype(BF16)

    def rows(k):
        return pl.ds(pl.multiple_of(k * 32, 32), 32)

    def out_copy(to):
        return remote(part.at[rows(to), :], got.at[me], s1.at[to], r1.at[me], (to, f))

    def own_copy():
        return pltpu.make_async_copy(part.at[rows(me), :], got.at[me], lsem)

    own_copy().start()

    def send(i, carry):
        out_copy(lax.rem(me + i, n)).start()
        return carry

    lax.fori_loop(1, n, send, 0)
    send_gin.start()
    own_copy().wait()

    def collect(i, total):
        src = lax.rem(me + n - i, n)
        remote(part.at[rows(src), :], got.at[src], s1.at[src], r1.at[src], (src, f)).wait_recv()
        return total + got[src].astype(F32)

    total = lax.fori_loop(1, n, collect, got[me].astype(F32))
    mine_b[...] = total.astype(BF16)
    full[rows(me), :] = mine_b[...]

    def share_copy(to):
        return remote(mine_b, full.at[rows(me), :], s2.at[to], r2.at[me], (to, f))

    def share(i, carry):
        share_copy(lax.rem(me + i, n)).start()
        return carry

    lax.fori_loop(1, n, share, 0)
    send_gin.wait_recv()
    gin_ref[:, pl.ds(pl.multiple_of((1 - chip) * 2048, 2048), 2048)] = gin_in[...]
    gw_ref[rows(me), :] = full[rows(me), :].astype(F32) * scale

    def take(i, carry):
        src = lax.rem(me + n - i, n)
        remote(mine_b, full.at[rows(src), :], s2.at[src], r2.at[src], (src, f)).wait_recv()
        gw_ref[rows(src), :] = full[rows(src), :].astype(F32) * scale
        return carry

    lax.fori_loop(1, n, take, 0)

    def drain(i, carry):
        to = lax.rem(me + i, n)
        out_copy(to).wait_send()
        share_copy(to).wait_send()
        return carry

    lax.fori_loop(1, n, drain, 0)
    for one in (send_far, send_sib, send_fwd, send_gin):
        one.wait_send()


def grads(scale, dp, x, xr, xs, w, wsib):
    n = 32
    return pl.pallas_call(
        functools.partial(grads_kernel, scale),
        out_shape=(
            jax.ShapeDtypeStruct((TOK, 4096), BF16),
            jax.ShapeDtypeStruct((1024, COLS), F32),
        ),
        in_specs=[VMEM] * 6,
        out_specs=[VMEM] * 2,
        scratch_shapes=[
            pltpu.VMEM((3, TOK, COLS), BF16),
            pltpu.VMEM((TOK, 2048), BF16),
            pltpu.VMEM((TOK, 2048), BF16),
            pltpu.VMEM((1024, COLS), BF16),
            pltpu.VMEM((n, 32, COLS), BF16),
            pltpu.VMEM((32, COLS), BF16),
            pltpu.VMEM((1024, COLS), BF16),
            pltpu.SemaphoreType.DMA((4,)),
            pltpu.SemaphoreType.DMA((4,)),
            pltpu.SemaphoreType.DMA((n,)),
            pltpu.SemaphoreType.DMA((n,)),
            pltpu.SemaphoreType.DMA((n,)),
            pltpu.SemaphoreType.DMA((n,)),
            pltpu.SemaphoreType.DMA,
        ],
        compiler_params=pltpu.CompilerParams(
            collective_id=2, has_side_effects=True, vmem_limit_bytes=56 * 2**20
        ),
        name="grads",
    )(dp, x, xr, xs, w, wsib)


def body(inputs, values, cotangent, weight, init_state, resets, dt_bias, decay_rate, skip):
    x = inputs[0]
    me = lax.axis_index("ctx")
    n = lax.axis_size("ctx")
    scale = 1.0 / math.sqrt(lax.axis_size("fsdp") * TOK * n)
    first = lax.dynamic_slice_in_dim(init_state[0], me * 4, 4, 0)
    first = first.reshape(OWN, STATE).T
    b, c, raw, wsib, xr, xs = project(x, weight)
    dp, gval = states(b, c, raw, values[0], cotangent[0], resets, dt_bias[None], decay_rate[None], skip[None], first)
    gin, gw = grads(scale, dp, x, xr, xs, weight, wsib)
    return (gin[None], gval[None], gw)


def solution(mesh):
    in_specs = (
        P("fsdp", "ctx", None),
        P("fsdp", "ctx", None),
        P("fsdp", "ctx", None),
        P("fsdp", None),
        P("fsdp", None, None),
        P("fsdp", "ctx"),
        P(),
        P(),
        P(),
    )
    out_specs = (P("fsdp", "ctx", None), P("fsdp", "ctx", None), P("fsdp", None))
    return jax.shard_map(body, mesh=mesh, in_specs=in_specs, out_specs=out_specs, check_vma=False)
```

time: 2290 us -> 218 us (0.10)
  waiting for transfers between devices: 1890 us -> 0 us
  Pallas kernels: 0 us -> 201 us
  matrix products: 104 us -> 0 us
  other arithmetic: 101 us -> 0 us
  blocking collectives: 83.1 us -> 0 us
  local copies, waits for them, and re-layouts: 81.6 us -> 14.3 us
    all_gather x3 -> x0, waiting for transfers between devices: 1440 us -> none  [the longest x2 1370 us: prefix(): gathered = jax.tree.map(lambda a: lax.all_gather(a, axis), part)]
    psum x1 -> x0, waiting for transfers between devices: 314 us -> none  [body(): grad_w = lax.psum(own_rows, 'ctx')]
    pallas_call x0 -> x3, Pallas kernels: none -> 201 us  [the longest x1 96.6 us: grads(): pl.pallas_call(functools.partial(grads_kernel, scale), out_shape=(jax.Sha...]
    reduce_scatter x1 -> x0, waiting for transfers between devices: 142 us -> none  [body(): lax.psum_scatter(jnp.einsum('qd,qc->dc', token_rows, d_proj, preferred_el...]
    dot_general x63 -> x0, matrix products: 83.7 us -> none  [the longest x16 21.2 us: group_terms(): jnp.einsum('kts,skp->tkp', mixed, disc_group, preferred_element_type=jnp....]
    all_gather x1 -> x0, blocking collectives: 83.1 us -> none  [prefix(): gathered = jax.tree.map(lambda a: lax.all_gather(a, axis), part)]
    add x33 -> x0, other arithmetic: 73.9 us -> none  [the longest x31 65.3 us: chain_backward(): return (earlier[0] * later[0], later[1] + later[0][:, None] * earlier[1])]
  transfers between devices with their start and end apart: 5 -> 0, of which waited for: 5 -> 0; matrix products, arithmetic and copies ran while one was open for 3% -> 0% of each run, Pallas kernels for 0% -> 0%
where the time goes in v1:
time: 218 us; the launch traced here: 216 us
  Pallas kernels  201 us (92%)
  local copies, waits for them, and re-layouts  14.3 us (7%)
    pallas_call x1, Pallas kernels, grads(): pl.pallas_call(functools.partial(grads_kernel, scale), out_shape=(jax.Sha...  96.6 us
    pallas_call x1, Pallas kernels, states(): pl.pallas_call(states_kernel, out_shape=(jax.ShapeDtypeStruct((TOK, COLS)...  76.1 us
    pallas_call x1, Pallas kernels, project(): pl.pallas_call(project_kernel, out_shape=shapes, in_specs=[VMEM] * 2, out...  28.1 us
    unnamed x23, local copies, waits for them, and re-layouts  13.4 us

profile of v1, /device:TPU:0, one launch (start us, length us, event | category | flops | bytes accessed | tf_op | source)
XLA Modules:
  0.0 215.8 jit_solution(13237719164680744806)
XLA Ops:
  0.6 0.0 copy-start
  0.6 1.2 copy-done
  1.9 0.1 reshape.11
  2.0 0.7 copy.12
  2.7 0.0 copy-start.1
  2.7 1.2 copy-done.1
  3.9 28.1 %project.1 = (bf16[8,128,64]{2,1,0:T(8,128)(2,1)S(1)}, bf16[8,128,64]{2,1,0:T(8,128)(2,1)S(1)}, f32[128,128]{1,0:T(8,128)S(1)}, bf16[1024,1152]{1,0:T(8,128)(2,1...) custom-call(bf16[128,4096]{1,0:T(8,128)(2,1)S(1)} %bitcast.10, bf16[1024,1152]{1,0:T(8,128)(2,1)} %w_ref.3), custom_call_target="tpu_custom_call" | custom-call | tf_op jit(solution)/shard_map/project/pallas_call | solution.py:116
  32.1 0.0 copy-start.2
  32.1 1.4 copy-done.2
  33.5 0.0 copy-start.3
  33.5 0.8 copy-done.3
  34.3 0.0 copy-start.4
  34.3 0.8 copy-done.4
  35.1 0.0 copy-start.5
  35.1 0.7 copy-done.5
  35.8 0.0 copy-start.6
  35.8 0.7 copy-done.6
  36.5 0.0 copy-start.7
  36.5 0.6 copy-done.7
  37.1 76.1 %states.1 = (bf16[128,1152]{1,0:T(8,128)(2,1)}, bf16[128,8192]{1,0:T(8,128)(2,1)}) custom-call(bf16[8,128,64]{2,1,0:T(8,128)(2,1)} %copy-done.5, bf16[8,128,64]{2,1,0:T(8,128)(2,1)} %copy-done.6, f32[128,128]{1,0:T(8,128)} %copy-done.7, bf16[128,8192]{1,0:T(8,128)(2,1)} %bitcast.11, bf16[128,8192]{1,0:T(8,128)(2,1)} %bitcast.12, s32[1,128]{1,0:T(1,128)} %resets_ref.1, ...), custom_call_target="tpu_custom_call" | custom-call | tf_op jit(solution)/shard_map/states/pallas_call | solution.py:381
  113.2 0.0 copy-start.9
  113.2 96.6 %grads.1 = (bf16[128,4096]{1,0:T(8,128)(2,1)}, f32[1024,1152]{1,0:T(8,128)}) custom-call(bf16[128,1152]{1,0:T(8,128)(2,1)} %get-tuple-element.16.dp_ref, bf16[128,4096]{1,0:T(8,128)(2,1)} %bitcast.9, bf16[128,2048]{1,0:T(8,128)(2,1)} %copy-done.3, bf16[2,128,1024]{2,1,0:T(8,128)(2,1)} %copy-done.4, bf16[1024,1152]{1,0:T(8,128)(2,1)} %w_ref.3, ...), custom_call_target="tpu_custom_call" | custom-call | tf_op jit(solution)/shard_map/grads/pallas_call | solution.py:523
  209.8 0.0 copy-start.8
  209.8 2.4 %copy.16 = bf16[1,128,4096]{2,1,0:T(8,128)(2,1)} copy(bf16[1,128,4096]{2,1,0:T(8,128)(2,1)} %bitcast.14) | data formatting | bytes 2097152
  212.3 0.0 copy-done.9
  212.3 1.3 copy.17
  213.6 0.0 copy-done.8
  213.6 2.2 %copy.18 = f32[1024,1152]{1,0:T(8,128)} copy(f32[1024,1152]{1,0:T(8,128)S(1)} %copy-done.8) | data formatting | bytes 9437184
  (1 shorter events, 0.0 us)
Async XLA Ops:
  0.6 1.2 copy-start
  2.7 1.2 copy-start.1
  32.1 1.4 copy-start.2
  33.5 0.8 copy-start.3
  34.3 0.8 copy-start.4
  35.1 0.7 copy-start.5
  35.8 0.7 copy-start.6
  36.5 0.6 copy-start.7
  113.2 99.0 %copy-start.9 = (bf16[128,8192]{1,0:T(8,128)(2,1)S(1)}, bf16[128,8192]{1,0:T(8,128)(2,1)}, u32[]{:S(2)}) copy-start(bf16[128,8192]{1,0:T(8,128)(2,1)} %get-tuple-element.21) | copy-start | bytes 6291460
  209.8 3.8 %copy-start.8 = (f32[1024,1152]{1,0:T(8,128)S(1)}, f32[1024,1152]{1,0:T(8,128)}, u32[]{:S(2)}) copy-start(f32[1024,1152]{1,0:T(8,128)} %get-tuple-element.28) | copy-start | bytes 14155780

commit v2 on v1

v2 whole, which is shorter than its diff:
```python
import functools
import math

import jax
import jax.numpy as jnp
from jax import lax
from jax.experimental import pallas as pl
from jax.experimental.pallas import tpu as pltpu
from jax.sharding import PartitionSpec as P

MESH = pl.DeviceIdType.MESH
F32 = jnp.float32
BF16 = jnp.bfloat16
TOK = 128
HEADS = 128
GROUPS = 8
STATE = 64
WIDE = 1024
COLS = 1152
MSG = 144
OWN = 256
VMEM = pl.BlockSpec(memory_space=pltpu.VMEM)


def nn(a, b):
    return lax.dot_general(a, b, (((1,), (0,)), ((), ())), preferred_element_type=F32)


def nt(a, b):
    return lax.dot_general(a, b, (((1,), (1,)), ((), ())), preferred_element_type=F32)


def tn(a, b):
    return lax.dot_general(a, b, (((0,), (0,)), ((), ())), preferred_element_type=F32)


def split2(x):
    high = x.astype(BF16)
    return high, (x - high.astype(F32)).astype(BF16)


def split3(x):
    high, rest = x.astype(BF16), None
    rest = x - high.astype(F32)
    mid = rest.astype(BF16)
    return high, mid, (rest - mid.astype(F32)).astype(BF16)


def exact(mat, x):
    return sum(nn(mat, part) for part in split3(x))


def remote(src, dst, ssem, rsem, to):
    return pltpu.make_async_remote_copy(
        src_ref=src, dst_ref=dst, send_sem=ssem, recv_sem=rsem, device_id=to, device_id_type=MESH
    )


def block_masks(resets_ref):
    flags = resets_ref[...].astype(F32)
    row = lax.broadcasted_iota(jnp.int32, (TOK, TOK), 0)
    col = lax.broadcasted_iota(jnp.int32, (TOK, TOK), 1)
    seg_col = jnp.sum(jnp.where(col <= row, flags, 0.0), axis=1, keepdims=True)
    flag_col = jnp.sum(jnp.where(col == row, flags, 0.0), axis=1, keepdims=True)
    seg_row = jnp.sum(jnp.where(row <= col, flag_col, 0.0), axis=0, keepdims=True)
    valid = (col <= row) & (seg_col == seg_row)
    return row, col, valid, seg_col


def spread_matrix(g):
    head = lax.rem(lax.broadcasted_iota(jnp.int32, (256, WIDE), 0), 128)
    lane = lax.broadcasted_iota(jnp.int32, (256, WIDE), 1) // STATE
    return jnp.where(head == lane + 16 * g, 1.0, 0.0).astype(BF16)


def gather_matrix(g):
    lane = lax.broadcasted_iota(jnp.int32, (WIDE, HEADS), 0) // STATE
    head = lax.broadcasted_iota(jnp.int32, (WIDE, HEADS), 1)
    return jnp.where(head == lane + 16 * g, 1.0, 0.0).astype(BF16)


def per_head(x, mat):
    high, low = split2(x)
    return nn(high, mat) + nn(low, mat)


def layer_kernel(x_hbm, w_hbm, val_hbm, cot_hbm, init_hbm, resets_ref, bias_ref, rate_ref, skip_ref,
                 gin_hbm, gval_hbm, gw_hbm,
                 x_ref, w_ref, wsib_ref, xall, xo_ref, own_ref, away_ref, put_b, put_c, put_raw,
                 got_b, got_c, got_raw, b_ref, c_ref, val_ref, cot_ref, init_ref,
                 disc_ref, wgt_ref, rc_ref, step_ref, skipx_ref, totx_ref, dd_ref, logt_ref, logd_ref,
                 dlog_ref, dstep_ref, db_ref, dc_ref, out_ref, in_ref, back_ref, home_ref,
                 dall, gin_ref, ginfar_ref, part, ra1, rb1, a1, b1, ra2, rb2, s3, r3, f3, g3, a32, b32, a128, b128,
                 ssem, rsem, lsem, s1, r1, s2, r2):
    n = lax.axis_size("ctx")
    me, f = lax.axis_index("ctx"), lax.axis_index("fsdp")
    core, chip = lax.rem(f, 2), f // 2
    my_row, my_x = me // 4, lax.rem(me, 4)
    my_z, my_y = lax.rem(my_row, 4), my_row // 4
    sib = (me, f + 1 - 2 * core)
    far = (me, lax.rem(f + 2, 4))
    pair = (lax.rem(me + 16, n), f)
    bar = pltpu.get_barrier_semaphore()
    for to in (far, sib):
        pl.semaphore_signal(bar, inc=1, device_id=to, device_id_type=MESH)

    def greet(i, carry):
        pl.semaphore_signal(bar, inc=1, device_id=(lax.rem(me + i, n), f), device_id_type=MESH)
        return carry

    lax.fori_loop(1, n, greet, 0)
    mine = pl.multiple_of(core * 1024, 1024)
    other = pl.multiple_of((1 - core) * 1024, 1024)
    base = pl.multiple_of(chip * 2048, 2048)
    far_base = pl.multiple_of((1 - chip) * 2048, 2048)
    own_at = pl.multiple_of(base + mine, 1024)
    other_at = pl.multiple_of(base + other, 1024)
    init_at = pl.multiple_of((me // 4) * 16, 16)
    loads = [
        pltpu.make_async_copy(w_hbm, w_ref, lsem.at[0]),
        pltpu.make_async_copy(x_hbm, x_ref, lsem.at[1]),
        pltpu.make_async_copy(cot_hbm, cot_ref, lsem.at[2]),
        pltpu.make_async_copy(val_hbm, val_ref, lsem.at[3]),
        pltpu.make_async_copy(init_hbm.at[pl.ds(init_at, 16), :], init_ref, lsem.at[4]),
    ]
    for one in loads:
        one.start()
    pl.semaphore_wait(bar, n + 1)

    def link(k, source, target, to):
        return remote(source, target, ssem.at[k], rsem.at[k], to)

    send_x0 = link(0, x_hbm.at[:, pl.ds(pl.multiple_of(far_base + mine, 1024), 1024)], xall.at[pl.ds(128, 128), :], far)
    send_x1 = link(1, x_hbm.at[:, pl.ds(pl.multiple_of(far_base + other, 1024), 1024)], xo_ref, far)
    send_w = link(2, w_hbm, wsib_ref, sib)
    send_xo = link(3, x_hbm.at[:, pl.ds(other_at, 1024)], xall.at[pl.ds(256, 128), :], sib)
    for one in (send_x0, send_x1, send_w, send_xo):
        one.start()
    row, col, valid, seg_col = block_masks(resets_ref)
    loads[0].wait()
    loads[1].wait()
    xall[:128, :] = x_ref[:, pl.ds(own_at, 1024)]
    own_ref[...] = nn(xall[:128, :], w_ref[...])
    send_w.wait_recv()
    own_ref[...] += nn(x_ref[:, pl.ds(other_at, 1024)], wsib_ref[...])
    send_x0.wait_recv()
    away_ref[...] = nn(xall[128:256, :], w_ref[...])
    send_x1.wait_recv()
    send_fwd = link(4, xo_ref, xall.at[pl.ds(384, 128), :], sib)
    send_fwd.start()
    put_raw[...] = away_ref[:, 1024:] + nn(xo_ref[...], wsib_ref[:, 1024:])
    send_raw = link(5, put_raw, got_raw, far)
    send_raw.start()
    put_b[...] = (away_ref[:, :512] + nn(xo_ref[...], wsib_ref[:, :512])).astype(BF16)
    send_b = link(6, put_b, got_b, far)
    send_b.start()
    put_c[...] = (away_ref[:, 512:1024] + nn(xo_ref[...], wsib_ref[:, 512:1024])).astype(BF16)
    send_c = link(7, put_c, got_c, far)
    send_c.start()

    send_raw.wait_recv()
    raw = own_ref[:, 1024:] + got_raw[...] + bias_ref[...]
    step = jnp.maximum(raw, 0.0) + jnp.log1p(jnp.exp(-jnp.abs(raw)))
    low_tri = jnp.where(col <= row, 1.0, 0.0).astype(BF16)
    log_decay = exact(low_tri, -rate_ref[...] * step)
    final = log_decay[TOK - 1:, :]
    last_seg = seg_col[TOK - 1:, :]
    tail = jnp.where(seg_col == last_seg, jnp.exp(final - log_decay), 0.0)
    reach = jnp.where(seg_col == 0.0, jnp.exp(log_decay), 0.0)
    total = jnp.where(last_seg == 0.0, jnp.exp(final), 0.0)
    logd_ref[...] = log_decay
    logt_ref[...] = jnp.transpose(log_decay)
    few = lax.broadcasted_iota(jnp.int32, (16, HEADS), 0)
    extra = jnp.where(few < 8, skip_ref[...], total)
    stack = jnp.concatenate([step, tail, reach, extra], axis=0)
    stack = jnp.concatenate(split2(stack), axis=1)
    loads[2].wait()
    loads[3].wait()
    send_b.wait_recv()
    full_b = (own_ref[:, :512] + got_b[...].astype(F32)).astype(BF16)
    for g in range(GROUPS):
        b_ref[g] = full_b[:, g * STATE:(g + 1) * STATE]
    send_c.wait_recv()
    full_c = (own_ref[:, 512:1024] + got_c[...].astype(F32)).astype(BF16)
    for g in range(GROUPS):
        c_ref[g] = full_c[:, g * STATE:(g + 1) * STATE]

    def wide(g):
        return pl.ds(pl.multiple_of(g * WIDE, WIDE), WIDE)

    def out_copy(to):
        return remote(out_ref.at[to], in_ref.at[me], s1.at[to], r1.at[me], (to, f))

    def own_copy():
        return pltpu.make_async_copy(out_ref.at[me], in_ref.at[me], lsem.at[5])

    def produce(i, carry):
        g = lax.rem(my_row + i, GROUPS)
        spread = nn(stack, spread_matrix(g))
        step_x = spread[:TOK]
        cot = cot_ref[:, wide(g)].astype(F32)
        disc = (step_x * val_ref[:, wide(g)].astype(F32)).astype(BF16)
        wgt = (spread[TOK:2 * TOK] * disc.astype(F32)).astype(BF16)
        rc = (spread[2 * TOK:3 * TOK] * cot).astype(BF16)
        step_ref[g] = step_x
        skipx_ref[g] = spread[3 * TOK:3 * TOK + 8]
        totx_ref[g] = spread[3 * TOK + 8:3 * TOK + 16]
        disc_ref[g] = disc
        wgt_ref[g] = wgt
        rc_ref[g] = rc
        local = tn(b_ref[g], wgt).astype(BF16)
        first = tn(c_ref[g], rc).astype(BF16)
        tot = spread[3 * TOK + 8:3 * TOK + 9]
        high, low = split2(tot)
        which = lax.broadcasted_iota(jnp.int32, (16, WIDE), 0)
        tots = jnp.where(which == 0, high.astype(F32), jnp.where(which == 1, low.astype(F32), 0.0)).astype(BF16)
        for j in range(4):
            to = g * 4 + j
            lanes = slice(j * OWN, (j + 1) * OWN)
            out_ref[to, :64, :] = local[:, lanes]
            out_ref[to, 64:128, :] = first[:, lanes]
            out_ref[to, 128:, :] = tots[:, lanes]
        for j in range(4):
            to = g * 4 + lax.rem(my_x + j, 4)

            @pl.when(to != me)
            def _():
                out_copy(to).start()

            @pl.when(to == me)
            def _():
                own_copy().start()

        return carry

    lax.fori_loop(0, GROUPS, produce, 0)

    dlog_ref[...] = jnp.zeros_like(dlog_ref)
    half = lax.broadcasted_iota(jnp.int32, (1, TOK), 1) < STATE
    left = jnp.where(half, 1.0, 0.0)
    left_b = left.astype(BF16)
    right_b = (1.0 - left).astype(BF16)
    bad = jnp.where(valid, 0.0, 1.0)

    def inside(g, carry):
        b, c = b_ref[g], c_ref[g]
        scores = nt(c, b)
        logs = pltpu.roll(logd_ref[...], lax.rem(HEADS - 16 * g, HEADS), 1)
        d_scores = jnp.zeros((TOK, TOK), F32)
        errs = []
        for q in range(8):
            lanes = pl.ds(pl.multiple_of(g * WIDE + q * 128, 128), 128)
            cot_p = cot_ref[:, lanes]
            disc_p = disc_ref[g, :, q * 128:(q + 1) * 128]
            stacked = jnp.concatenate([disc_p * left_b, disc_p * right_b], axis=0)
            d_mixed = nt(cot_p, stacked)
            mixed = []
            for k in range(2):
                head = 2 * q + k
                span = logs[:, head:head + 1] - logt_ref[pl.ds(g * 16 + head, 1), :]
                weights = jnp.exp(jnp.where(valid, span, -1e30))
                d_scores += d_mixed[:, k * TOK:(k + 1) * TOK] * weights
                mixed.append((weights * scores).astype(BF16))
            mixed = jnp.concatenate(mixed, axis=1)
            inner = nn(mixed, stacked)
            both = tn(mixed, cot_p)
            dd = both[:TOK] * left + both[TOK:] * (1.0 - left)
            dd_ref[g, :, q * 128:(q + 1) * 128] = dd.astype(BF16)
            errs.append(cot_p.astype(F32) * inner - disc_p.astype(F32) * dd)
        dlog_ref[...] += per_head(jnp.concatenate(errs, axis=1), gather_matrix(g))
        ds = d_scores.astype(BF16)
        dc_ref[g] = nn(ds, b)
        db_ref[g] = tn(ds, c)
        return carry

    lax.fori_loop(0, GROUPS, inside, 0)

    loads[4].wait()
    pick_row = lax.broadcasted_iota(jnp.int32, (16, 16), 0)
    pick_col = lax.broadcasted_iota(jnp.int32, (16, 16), 1)
    pick = jnp.where(pick_col == pick_row + 4 * my_x, 1.0, 0.0).astype(BF16)
    picked = nn(pick, init_ref[...])
    turned = [picked[h:h + 1, i * 128:(i + 1) * 128] for h in range(4) for i in range(32)]
    turned = jnp.transpose(jnp.concatenate(turned, axis=0)).astype(BF16)
    from_i = lax.broadcasted_iota(jnp.int32, (128, OWN), 0)
    to_p = lax.broadcasted_iota(jnp.int32, (128, OWN), 1)
    even = jnp.where(to_p == 2 * from_i, 1.0, 0.0).astype(BF16)
    odd = jnp.where(to_p == 2 * from_i + 1, 1.0, 0.0).astype(BF16)
    init_state = nn(turned[:64], even) + nn(turned[64:], odd)

    own_copy().wait()

    def arrive(i, carry):
        src = lax.rem(me + n - i, n)
        remote(out_ref.at[src], in_ref.at[src], s1.at[src], r1.at[src], (src, f)).wait_recv()
        return carry

    lax.fori_loop(1, n, arrive, 0)

    def lap_total(j):
        return jnp.sum(in_ref[j, 128:, :].astype(F32), axis=0, keepdims=True)

    def forward(j, state):
        back_ref[j, :64, :] = state.astype(BF16)
        return lap_total(j) * state + in_ref[j, :64, :].astype(F32)

    lax.fori_loop(0, n, forward, init_state)

    def backward(i, state):
        j = n - 1 - i
        back_ref[j, 64:, :] = state.astype(BF16)
        return in_ref[j, 64:128, :].astype(F32) + lap_total(j) * state

    lax.fori_loop(0, n, backward, jnp.zeros((STATE, OWN), F32))

    def back_copy(to):
        return remote(back_ref.at[to], home_ref.at[me], s2.at[to], r2.at[me], (to, f))

    def own_back():
        return pltpu.make_async_copy(back_ref.at[me], home_ref.at[me], lsem.at[6])

    def send_back(i, carry):
        g = lax.rem(my_row + i, GROUPS)
        for j in range(4):
            to = g * 4 + lax.rem(my_x + j, 4)

            @pl.when(to != me)
            def _():
                back_copy(to).start()

            @pl.when(to == me)
            def _():
                own_back().start()

        return carry

    lax.fori_loop(0, GROUPS, send_back, 0)
    own_back().wait()
    dstep_ref[...] = jnp.zeros_like(dstep_ref)

    def save(g):
        return pltpu.make_async_copy(disc_ref.at[g], gval_hbm.at[:, wide(g)], lsem.at[8 + g])

    def consume(i, carry):
        g = lax.rem(my_row + GROUPS - i, GROUPS)
        for j in range(4):
            src = g * 4 + j

            @pl.when(src != me)
            def _():
                remote(back_ref.at[src], home_ref.at[src], s2.at[src], r2.at[src], (src, f)).wait_recv()

        got = jnp.concatenate([home_ref[g * 4 + j] for j in range(4)], axis=1)
        start, end = got[:64], got[64:]
        b, c = b_ref[g], c_ref[g]
        rc, wgt, disc = rc_ref[g], wgt_ref[g], disc_ref[g].astype(F32)
        carried = nn(c, start)
        d_wgt = nn(b, end)
        dc_ref[g] += nt(rc, start)
        db_ref[g] += nt(wgt, end)
        pull = wgt.astype(F32) * d_wgt
        mat = gather_matrix(g)
        err = rc.astype(F32) * carried - pull
        ends = jnp.sum(pull, axis=0, keepdims=True)
        ends += totx_ref[g, :1, :] * jnp.sum(start.astype(F32) * end.astype(F32), axis=0, keepdims=True)
        at_end = lax.broadcasted_iota(jnp.int32, (TOK, WIDE), 0) == TOK - 1
        err = err + jnp.where(at_end, ends, 0.0)
        dlog_ref[...] += per_head(err, mat)
        spread = nn(stack[TOK:2 * TOK], spread_matrix(g))
        d_disc = dd_ref[g].astype(F32) + spread * d_wgt
        val = val_ref[:, wide(g)].astype(F32)
        dstep_ref[...] += per_head(d_disc * val, mat)
        gval = skipx_ref[g, :1, :] * cot_ref[:, wide(g)].astype(F32) + step_ref[g] * d_disc
        disc_ref[g] = gval.astype(BF16)
        save(g).start()
        return carry

    lax.fori_loop(0, GROUPS, consume, 0)
    up_tri = jnp.where(col >= row, 1.0, 0.0).astype(BF16)
    d_inc = exact(up_tri, dlog_ref[...])
    d_step = dstep_ref[...] - rate_ref[...] * d_inc
    d_raw = d_step / (1.0 + jnp.exp(-raw))
    pieces = [db_ref[g] for g in range(GROUPS)] + [dc_ref[g] for g in range(GROUPS)] + [d_raw]
    dall[:128, :] = jnp.concatenate(pieces, axis=1).astype(BF16)

    d_own = dall.at[pl.ds(0, 128), :]
    send_far = link(8, d_own, dall.at[pl.ds(128, 128), :], far)
    send_far.start()
    send_sib = link(9, d_own, dall.at[pl.ds(256, 128), :], sib)
    send_sib.start()
    gin_ref[:, pl.ds(mine, 1024)] = nt(dall[:128, :], w_ref[...]).astype(BF16)
    gin_ref[:, pl.ds(other, 1024)] = nt(dall[:128, :], wsib_ref[...]).astype(BF16)
    save_gin = pltpu.make_async_copy(gin_ref, gin_hbm.at[:, pl.ds(base, 2048)], lsem.at[7])
    save_gin.start()
    send_far.wait_recv()
    send_dfwd = link(10, dall.at[pl.ds(128, 128), :], dall.at[pl.ds(384, 128), :], sib)
    send_dfwd.start()
    send_xo.wait_recv()
    send_fwd.wait_recv()
    send_sib.wait_recv()
    send_dfwd.wait_recv()

    def rows(at, count):
        return pl.ds(pl.multiple_of(at, count), count)

    def x_peer(x):
        return (me - my_x + x, f)

    def z_peer(z):
        return (me + 4 * (z - my_z), f)

    def exchange(k, peer, mine_at, source, target):
        copies = []
        for step_to in range(1, 4):
            to = lax.rem(mine_at + step_to, 4)
            copies.append(remote(source(to), target(mine_at), ssem.at[k + to], rsem.at[k + mine_at], peer(to)))
        return copies

    def landed(k, peer, mine_at, source, target):
        for step_to in range(1, 4):
            at = lax.rem(mine_at + step_to, 4)
            remote(source(at), target(at), ssem.at[k + at], rsem.at[k + at], peer(at)).wait_recv()

    def product(at):
        part[rows(at, 128), :] = tn(xall[:, rows(at, 128)], dall[...]).astype(BF16)

    a_first = (12, x_peer, my_x, lambda x: part.at[rows(128 * x, 128), :], lambda x: ra1.at[x])
    b_first = (16, z_peer, my_z, lambda z: part.at[rows(512 + 128 * z, 128), :], lambda z: rb1.at[z])
    a_sent, b_sent = exchange(*a_first), exchange(*b_first)
    for k in range(3):
        product(128 * lax.rem(my_x + k + 1, 4))
        a_sent[k].start()
        product(512 + 128 * lax.rem(my_z + k + 1, 4))
        b_sent[k].start()
    product(128 * my_x)
    product(512 + 128 * my_z)
    ginfar_ref[:, pl.ds(mine, 1024)] = nt(dall[128:256, :], w_ref[...]).astype(BF16)
    ginfar_ref[:, pl.ds(other, 1024)] = nt(dall[128:256, :], wsib_ref[...]).astype(BF16)
    send_gin = link(11, ginfar_ref, gin_hbm.at[:, pl.ds(base, 2048)], far)
    send_gin.start()
    sent = a_sent + b_sent

    def summed(first, got, at):
        total = first.astype(F32)
        for step_to in range(1, 4):
            total += got[lax.rem(at + step_to, 4)].astype(F32)
        return total

    a_second = (20, z_peer, my_z, lambda z: a1.at[rows(32 * z, 32), :], lambda z: ra2.at[z])
    b_second = (24, x_peer, my_x, lambda x: b1.at[rows(32 * x, 32), :], lambda x: rb2.at[x])
    landed(*a_first)
    a1[...] = summed(part[rows(128 * my_x, 128), :], ra1, my_x).astype(BF16)
    a_sent = exchange(*a_second)
    for one in a_sent:
        one.start()
    landed(*b_first)
    b1[...] = summed(part[rows(512 + 128 * my_z, 128), :], rb1, my_z).astype(BF16)
    b_sent = exchange(*b_second)
    for one in b_sent:
        one.start()
    sent += a_sent + b_sent
    landed(*a_second)
    a2 = summed(a1[rows(32 * my_z, 32), :], ra2, my_z)
    landed(*b_second)
    b2 = summed(b1[rows(32 * my_x, 32), :], rb2, my_x)
    upper = jnp.where(my_y == 0, 1.0, 0.0)
    keep_a = a2[:16] * upper + a2[16:] * (1.0 - upper)
    keep_b = b2[:16] * upper + b2[16:] * (1.0 - upper)
    give_a = a2[:16] * (1.0 - upper) + a2[16:] * upper
    give_b = b2[:16] * (1.0 - upper) + b2[16:] * upper
    s3[...] = jnp.concatenate([give_a, give_b], axis=0).astype(BF16)
    third = link(28, s3, r3, pair)
    third.start()
    third.wait_recv()
    f3[...] = (jnp.concatenate([keep_a, keep_b], axis=0) + r3[...].astype(F32)).astype(BF16)
    fourth = link(29, f3, g3, pair)
    fourth.start()
    at_y, at_not = rows(16 * my_y, 16), rows(16 * (1 - my_y), 16)
    a32[at_y, :] = f3[:16, :]
    b32[at_y, :] = f3[16:, :]
    fourth.wait_recv()
    a32[at_not, :] = g3[:16, :]
    b32[at_not, :] = g3[16:, :]
    a_fifth = (30, z_peer, my_z, lambda z: a32, lambda z: a128.at[rows(32 * z, 32), :])
    b_fifth = (34, x_peer, my_x, lambda x: b32, lambda x: b128.at[rows(32 * x, 32), :])
    a_sent, b_sent = exchange(*a_fifth), exchange(*b_fifth)
    for one in a_sent + b_sent:
        one.start()
    sent += [third, fourth] + a_sent + b_sent
    a128[rows(32 * my_z, 32), :] = a32[...]
    b128[rows(32 * my_x, 32), :] = b32[...]
    a_last = (38, x_peer, my_x, lambda x: a128, lambda x: gw_hbm.at[rows(128 * x, 128), :])
    b_last = (42, z_peer, my_z, lambda z: b128, lambda z: gw_hbm.at[rows(512 + 128 * z, 128), :])
    landed(*a_fifth)
    a_sent = exchange(*a_last)
    for one in a_sent:
        one.start()
    landed(*b_fifth)
    b_sent = exchange(*b_last)
    for one in b_sent:
        one.start()
    sent += a_sent + b_sent
    keep = [
        pltpu.make_async_copy(a128, gw_hbm.at[rows(128 * my_x, 128), :], lsem.at[16]),
        pltpu.make_async_copy(b128, gw_hbm.at[rows(512 + 128 * my_z, 128), :], lsem.at[17]),
    ]
    for one in keep:
        one.start()

    def drain(i, carry):
        to = lax.rem(me + i, n)
        out_copy(to).wait_send()
        back_copy(to).wait_send()
        return carry

    lax.fori_loop(1, n, drain, 0)
    for one in (send_x0, send_x1, send_w, send_xo, send_fwd, send_raw, send_b, send_c,
                send_far, send_sib, send_dfwd, send_gin):
        one.wait_send()
    send_gin.wait_recv()
    save_gin.wait()

    def saved(g, carry):
        save(g).wait()
        return carry

    lax.fori_loop(0, GROUPS, saved, 0)
    for one in keep:
        one.wait()
    landed(*a_last)
    landed(*b_last)
    for one in sent:
        one.wait_send()


def layer(x, w, val, cot, init, resets, bias, rate, skip):
    n = 32
    slab = (GROUPS, TOK, WIDE)
    hbm = pl.BlockSpec(memory_space=pl.ANY)
    vm = pltpu.VMEM
    dma = pltpu.SemaphoreType.DMA
    return pl.pallas_call(
        layer_kernel,
        out_shape=(
            jax.ShapeDtypeStruct((TOK, 4096), BF16),
            jax.ShapeDtypeStruct((TOK, GROUPS * WIDE), BF16),
            jax.ShapeDtypeStruct((1024, COLS), BF16),
        ),
        in_specs=[hbm] * 5 + [VMEM] * 4,
        out_specs=[hbm] * 3,
        scratch_shapes=[
            vm((TOK, 4096), BF16),
            vm((1024, COLS), BF16),
            vm((1024, COLS), BF16),
            vm((4 * TOK, 1024), BF16),
            vm((TOK, 1024), BF16),
            vm((TOK, COLS), F32),
            vm((TOK, COLS), F32),
            vm((TOK, 512), BF16),
            vm((TOK, 512), BF16),
            vm((TOK, HEADS), F32),
            vm((TOK, 512), BF16),
            vm((TOK, 512), BF16),
            vm((TOK, HEADS), F32),
            vm((GROUPS, TOK, STATE), BF16),
            vm((GROUPS, TOK, STATE), BF16),
            vm((TOK, GROUPS * WIDE), BF16),
            vm((TOK, GROUPS * WIDE), BF16),
            vm((16, 4096), BF16),
            vm(slab, BF16),
            vm(slab, BF16),
            vm(slab, BF16),
            vm(slab, F32),
            vm((GROUPS, 8, WIDE), F32),
            vm((GROUPS, 8, WIDE), F32),
            vm(slab, BF16),
            vm((HEADS, TOK), F32),
            vm((TOK, HEADS), F32),
            vm((TOK, HEADS), F32),
            vm((TOK, HEADS), F32),
            vm((GROUPS, TOK, STATE), F32),
            vm((GROUPS, TOK, STATE), F32),
            vm((n, MSG, OWN), BF16),
            vm((n, MSG, OWN), BF16),
            vm((n, 128, OWN), BF16),
            vm((n, 128, OWN), BF16),
            vm((4 * TOK, COLS), BF16),
            vm((TOK, 2048), BF16),
            vm((TOK, 2048), BF16),
            vm((1024, COLS), BF16),
            vm((4, 128, COLS), BF16),
            vm((4, 128, COLS), BF16),
            vm((128, COLS), BF16),
            vm((128, COLS), BF16),
            vm((4, 32, COLS), BF16),
            vm((4, 32, COLS), BF16),
            vm((32, COLS), BF16),
            vm((32, COLS), BF16),
            vm((32, COLS), BF16),
            vm((32, COLS), BF16),
            vm((32, COLS), BF16),
            vm((32, COLS), BF16),
            vm((128, COLS), BF16),
            vm((128, COLS), BF16),
            dma((46,)),
            dma((46,)),
            dma((18,)),
            dma((n,)),
            dma((n,)),
            dma((n,)),
            dma((n,)),
        ],
        compiler_params=pltpu.CompilerParams(
            collective_id=0, has_side_effects=True, vmem_limit_bytes=60 * 2**20
        ),
        name="layer",
    )(x, w, val, cot, init, resets, bias, rate, skip)


def body(inputs, values, cotangent, weight, init_state, resets, dt_bias, decay_rate, skip):
    scale = 1.0 / math.sqrt(lax.axis_size("fsdp") * TOK * lax.axis_size("ctx"))
    gin, gval, gw = layer(inputs[0], weight, values[0], cotangent[0], init_state[0], resets,
                          dt_bias[None], decay_rate[None], skip[None])
    return (gin[None], gval[None], gw.astype(F32) * scale)


def solution(mesh):
    in_specs = (
        P("fsdp", "ctx", None),
        P("fsdp", "ctx", None),
        P("fsdp", "ctx", None),
        P("fsdp", None),
        P("fsdp", None, None),
        P("fsdp", "ctx"),
        P(),
        P(),
        P(),
    )
    out_specs = (P("fsdp", "ctx", None), P("fsdp", "ctx", None), P("fsdp", None))
    return jax.shard_map(body, mesh=mesh, in_specs=in_specs, out_specs=out_specs, check_vma=False)
```

time: 218 us -> 166 us (0.76)
  Pallas kernels: 201 us -> 157 us
  local copies, waits for them, and re-layouts: 14.3 us -> 3.29 us
  other arithmetic: 0 us -> 4.24 us
    pallas_call x3 -> x1, Pallas kernels: 201 us -> 157 us  [layer(): pl.pallas_call(layer_kernel, out_shape=(jax.ShapeDtypeStruct((TOK, 4096),...]
    unnamed x23 -> x6, local copies, waits for them, and re-layouts: 13.4 us -> 3.29 us
    mul x0 -> x1, other arithmetic: none -> 4.24 us  [body(): return (gin[None], gval[None], gw.astype(F32) * scale)]
where the time goes in v2:
time: 166 us
  Pallas kernels  157 us (95%)
  other arithmetic  4.24 us (3%)
  local copies, waits for them, and re-layouts  3.29 us (2%)
    pallas_call x1, Pallas kernels, layer(): pl.pallas_call(layer_kernel, out_shape=(jax.ShapeDtypeStruct((TOK, 4096),...  157 us
    mul x1, other arithmetic, body(): return (gin[None], gval[None], gw.astype(F32) * scale)  4.24 us

profile of v2, /device:TPU:0, one launch (start us, length us, event | category | flops | bytes accessed | tf_op | source)
XLA Modules:
  0.0 165.6 jit_solution(300678993200759335)
XLA Ops:
  0.6 157.4 %layer.1 = (bf16[128,4096]{1,0:T(8,128)(2,1)}, bf16[128,8192]{1,0:T(8,128)(2,1)}, bf16[1024,1152]{1,0:T(8,128)(2,1)}) custom-call(bf16[128,4096]{1,0:T(8,128)(2,1)} %bitcast.12, bf16[1024,1152]{1,0:T(8,128)(2,1)} %w_hbm.1, bf16[128,8192]{1,0:T(8,128)(2,1)} %bitcast.9, bf16[128,8192]{1,0:T(8,128)(2,1)} %bitcast.10, bf16[128,4096]{1,0:T(8,128)(2,1)} %bitcast.13, ...), custom_call_target="tpu_custom_call" | custom-call | tf_op jit(solution)/shard_map/layer/pallas_call | solution.py:542
  158.1 0.0 copy-start.1
  158.1 4.2 %convert_multiply_fusion = f32[1024,1152]{1,0:T(8,128)} fusion(bf16[1024,1152]{1,0:T(8,128)(2,1)} %get-tuple-element.8), kind=kLoop, calls=%fused_computation | loop fusion | flops 2359296 | bytes 7077888 | tf_op jit(solution)/shard_map/mul | solution.py:624
  162.3 0.0 copy-done.1
  162.3 0.0 copy-start
  162.3 1.0 copy.14
  163.3 1.0 copy-done
  164.3 1.3 copy.15
Async XLA Ops:
  158.1 4.3 %copy-start.1 = (bf16[128,4096]{1,0:T(8,128)(2,1)S(1)}, bf16[128,4096]{1,0:T(8,128)(2,1)}, u32[]{:S(2)}) copy-start(bf16[128,4096]{1,0:T(8,128)(2,1)} %get-tuple-element.6) | copy-start | bytes 3145732
  162.3 2.0 %copy-start = (bf16[128,8192]{1,0:T(8,128)(2,1)S(1)}, bf16[128,8192]{1,0:T(8,128)(2,1)}, u32[]{:S(2)}) copy-start(bf16[128,8192]{1,0:T(8,128)(2,1)} %get-tuple-element.7) | copy-start | bytes 6291460

commit v3 on v2

v3 whole, which is shorter than its diff:
```python
import functools
import math

import jax
import jax.numpy as jnp
from jax import lax
from jax.experimental import pallas as pl
from jax.experimental.pallas import tpu as pltpu
from jax.sharding import PartitionSpec as P

MESH = pl.DeviceIdType.MESH
F32 = jnp.float32
BF16 = jnp.bfloat16
TOK = 128
HEADS = 128
GROUPS = 8
STATE = 64
WIDE = 1024
COLS = 1152
PAIRS = 4
OWN = 256
HALF = 128
SPLIT = 4
VMEM = pl.BlockSpec(memory_space=pltpu.VMEM)


def nn(a, b):
    return lax.dot_general(a, b, (((1,), (0,)), ((), ())), preferred_element_type=F32)


def nt(a, b):
    return lax.dot_general(a, b, (((1,), (1,)), ((), ())), preferred_element_type=F32)


def tn(a, b):
    return lax.dot_general(a, b, (((0,), (0,)), ((), ())), preferred_element_type=F32)


def split2(x):
    high = x.astype(BF16)
    return high, (x - high.astype(F32)).astype(BF16)


def split3(x):
    high, rest = x.astype(BF16), None
    rest = x - high.astype(F32)
    mid = rest.astype(BF16)
    return high, mid, (rest - mid.astype(F32)).astype(BF16)


def exact(mat, x):
    return sum(nn(mat, part) for part in split3(x))


def remote(src, dst, ssem, rsem, to):
    return pltpu.make_async_remote_copy(
        src_ref=src, dst_ref=dst, send_sem=ssem, recv_sem=rsem, device_id=to, device_id_type=MESH
    )


def block_masks(resets_ref):
    flags = resets_ref[...].astype(F32)
    row = lax.broadcasted_iota(jnp.int32, (TOK, TOK), 0)
    col = lax.broadcasted_iota(jnp.int32, (TOK, TOK), 1)
    seg_col = jnp.sum(jnp.where(col <= row, flags, 0.0), axis=1, keepdims=True)
    flag_col = jnp.sum(jnp.where(col == row, flags, 0.0), axis=1, keepdims=True)
    seg_row = jnp.sum(jnp.where(row <= col, flag_col, 0.0), axis=0, keepdims=True)
    valid = (col <= row) & (seg_col == seg_row)
    return row, col, valid, seg_col


def spread_matrix(g):
    head = lax.rem(lax.broadcasted_iota(jnp.int32, (256, WIDE), 0), 128)
    lane = lax.broadcasted_iota(jnp.int32, (256, WIDE), 1) // STATE
    return jnp.where(head == lane + 16 * g, 1.0, 0.0).astype(BF16)


def gather_matrix(g):
    lane = lax.broadcasted_iota(jnp.int32, (WIDE, HEADS), 0) // STATE
    head = lax.broadcasted_iota(jnp.int32, (WIDE, HEADS), 1)
    return jnp.where(head == lane + 16 * g, 1.0, 0.0).astype(BF16)


def per_head(x, mat):
    high, low = split2(x)
    return nn(high, mat) + nn(low, mat)


def layer_kernel(x_hbm, w_hbm, val_hbm, cot_hbm, init_hbm, resets_ref, bias_ref, rate_ref, skip_ref,
                 gin_hbm, gval_hbm, gw_hbm,
                 x_ref, w_ref, wsib_ref, xall, xo_ref, own_ref, away_ref, put_raw, got_raw, put_bc, got_bc,
                 b_ref, c_ref, val_ref, cot_ref, init_ref,
                 disc_ref, wgt_ref, rc_ref, step_ref, skipx_ref, totx_ref, dd_ref, logt_ref, logd_ref,
                 dlog_ref, dstep_ref, db_ref, dc_ref, out_ref, in_ref, back_ref, home_ref, tot_ref, tots_ref, lap_ref,
                 dall, gin_ref, ginfar_ref, part, ra1, rb1, a1, b1, ra2, rb2, fa, fb, a128, b128,
                 ssem, rsem, lsem, s1, r1, s2, r2, s3, r3, zsem, ysem):
    n = lax.axis_size("ctx")
    me, f = lax.axis_index("ctx"), lax.axis_index("fsdp")
    core, chip = lax.rem(f, 2), f // 2
    my_row, my_x = me // 4, lax.rem(me, 4)
    my_z, my_y = lax.rem(my_row, 4), my_row // 4
    sib = (me, f + 1 - 2 * core)
    far = (me, lax.rem(f + 2, 4))
    my_pair, my_eighth = me // 8, lax.rem(me, 8)
    my_plane = my_y * 4 + my_x
    bar = pltpu.get_barrier_semaphore()
    x_peers = [(me - my_x + lax.rem(my_x + k, 4), f) for k in range(1, 4)]
    z_peers = [(me + 4 * (lax.rem(my_z + k, 4) - my_z), f) for k in range(1, 4)]
    y_peer = (lax.rem(me + 16, n), f)
    direct = [far, sib] + x_peers + z_peers + [y_peer]
    for to in direct:
        pl.semaphore_signal(bar, inc=1, device_id=to, device_id_type=MESH)
    mine = pl.multiple_of(core * 1024, 1024)
    other = pl.multiple_of((1 - core) * 1024, 1024)
    base = pl.multiple_of(chip * 2048, 2048)
    far_base = pl.multiple_of((1 - chip) * 2048, 2048)
    own_at = pl.multiple_of(base + mine, 1024)
    other_at = pl.multiple_of(base + other, 1024)
    init_at = pl.multiple_of(my_pair * 16, 16)
    loads = [
        pltpu.make_async_copy(w_hbm, w_ref, lsem.at[0]),
        pltpu.make_async_copy(x_hbm, x_ref, lsem.at[1]),
        pltpu.make_async_copy(cot_hbm, cot_ref, lsem.at[2]),
        pltpu.make_async_copy(val_hbm, val_ref, lsem.at[3]),
        pltpu.make_async_copy(init_hbm.at[pl.ds(init_at, 16), :], init_ref.at[0], lsem.at[4]),
        pltpu.make_async_copy(init_hbm.at[pl.ds(init_at + 64, 16), :], init_ref.at[1], lsem.at[5]),
    ]
    for one in loads:
        one.start()
    pl.semaphore_wait(bar, len(direct))

    def link(k, source, target, to):
        return remote(source, target, ssem.at[k], rsem.at[k], to)

    send_x0 = link(0, x_hbm.at[:, pl.ds(pl.multiple_of(far_base + mine, 1024), 1024)], xall.at[pl.ds(128, 128), :], far)
    send_x1 = link(1, x_hbm.at[:, pl.ds(pl.multiple_of(far_base + other, 1024), 1024)], xo_ref, far)
    send_w = link(2, w_hbm, wsib_ref, sib)
    send_xo = link(3, x_hbm.at[:, pl.ds(other_at, 1024)], xall.at[pl.ds(256, 128), :], sib)
    for one in (send_x0, send_x1, send_w, send_xo):
        one.start()
    for to in z_peers:
        pl.semaphore_signal(zsem, inc=1, device_id=to, device_id_type=MESH)
    row, col, valid, seg_col = block_masks(resets_ref)
    loads[0].wait()
    loads[1].wait()
    xall[:128, :] = x_ref[:, pl.ds(own_at, 1024)]
    own_ref[...] = nn(xall[:128, :], w_ref[...])
    pl.semaphore_wait(zsem, 3)
    pl.semaphore_signal(ysem, inc=1, device_id=y_peer, device_id_type=MESH)
    send_w.wait_recv()
    own_ref[...] += nn(x_ref[:, pl.ds(other_at, 1024)], wsib_ref[...])
    send_x0.wait_recv()
    away_ref[...] = nn(xall[128:256, :], w_ref[...])
    send_x1.wait_recv()
    send_fwd = link(4, xo_ref, xall.at[pl.ds(384, 128), :], sib)
    send_fwd.start()
    put_raw[...] = away_ref[:, 1024:] + nn(xo_ref[...], wsib_ref[:, 1024:])
    send_raw = link(5, put_raw, got_raw, far)
    send_raw.start()

    def pair_cols(u):
        return pl.ds(pl.multiple_of(u * 128, 128), 128), pl.ds(pl.multiple_of(512 + u * 128, 128), 128)

    def bc_copy(u):
        return link(46 + u, put_bc.at[u], got_bc.at[u], far)

    def give(u, carry):
        for k, cols in enumerate(pair_cols(u)):
            product = away_ref[:, cols] + nn(xo_ref[...], wsib_ref[:, cols])
            put_bc[u, :, k * 128:(k + 1) * 128] = product.astype(BF16)
        bc_copy(u).start()
        return carry

    lax.fori_loop(0, PAIRS, give, 0)
    send_raw.wait_recv()
    raw = own_ref[:, 1024:] + got_raw[...] + bias_ref[...]
    step = jnp.maximum(raw, 0.0) + jnp.log1p(jnp.exp(-jnp.abs(raw)))
    low_tri = jnp.where(col <= row, 1.0, 0.0).astype(BF16)
    log_decay = exact(low_tri, -rate_ref[...] * step)
    final = log_decay[TOK - 1:, :]
    last_seg = seg_col[TOK - 1:, :]
    tail = jnp.where(seg_col == last_seg, jnp.exp(final - log_decay), 0.0)
    reach = jnp.where(seg_col == 0.0, jnp.exp(log_decay), 0.0)
    total = jnp.where(last_seg == 0.0, jnp.exp(final), 0.0)
    tot_ref[...] = jnp.broadcast_to(total, (8, HEADS))
    logd_ref[...] = log_decay
    logt_ref[...] = jnp.transpose(log_decay)
    few = lax.broadcasted_iota(jnp.int32, (16, HEADS), 0)
    extra = jnp.where(few < 8, skip_ref[...], total)
    stack = jnp.concatenate([step, tail, reach, extra], axis=0)
    stack = jnp.concatenate(split2(stack), axis=1)
    loads[2].wait()
    loads[3].wait()
    pl.semaphore_wait(ysem, 1)
    def wide(g):
        return pl.ds(pl.multiple_of(g * WIDE, WIDE), WIDE)

    def out_copy(h, to):
        return remote(out_ref.at[h, to], in_ref.at[h, me], s1.at[h, to], r1.at[h, me], (to, f))

    def own_copy(h):
        return pltpu.make_async_copy(out_ref.at[h, me], in_ref.at[h, me], lsem.at[18 + h])

    def tot_copy(to):
        return remote(tot_ref, tots_ref.at[me], s3.at[to], r3.at[me], (to, f))

    def to_eight(copy, own, h, u):
        for j in range(8):
            to = u * 8 + lax.rem(my_eighth + j, 8)

            @pl.when(to != me)
            def _():
                copy(h, to).start()

            @pl.when(to == me)
            def _():
                own(h).start()

    def all_blocks(copy, own, h):
        def block(i, carry):
            to_eight(copy, own, h, lax.rem(my_pair + i, PAIRS))
            return carry

        lax.fori_loop(0, PAIRS, block, 0)

    def all_sent(copy, h):
        def gone(i, carry):
            copy(h, lax.rem(me + i, n)).wait_send()
            return carry

        lax.fori_loop(1, n, gone, 0)

    for h in range(2):
        for u in (2 * h, 2 * h + 1):
            bc_copy(u).wait_recv()
            cols_b, cols_c = pair_cols(u)
            pair_b = (own_ref[:, cols_b] + got_bc[u, :, :128].astype(F32)).astype(BF16)
            pair_c = (own_ref[:, cols_c] + got_bc[u, :, 128:].astype(F32)).astype(BF16)
            for k in range(2):
                b_ref[2 * u + k] = pair_b[:, k * STATE:(k + 1) * STATE]
                c_ref[2 * u + k] = pair_c[:, k * STATE:(k + 1) * STATE]

        def produce(i, carry):
            block = lax.rem(my_pair + i, PAIRS)
            g = 4 * h + block
            spread = nn(stack, spread_matrix(g))
            step_x = spread[:TOK]
            cot = cot_ref[:, wide(g)].astype(F32)
            disc = (step_x * val_ref[:, wide(g)].astype(F32)).astype(BF16)
            wgt = (spread[TOK:2 * TOK] * disc.astype(F32)).astype(BF16)
            rc = (spread[2 * TOK:3 * TOK] * cot).astype(BF16)
            step_ref[g] = step_x
            skipx_ref[g] = spread[3 * TOK:3 * TOK + 8]
            totx_ref[g] = spread[3 * TOK + 8:3 * TOK + 16]
            disc_ref[g] = disc
            wgt_ref[g] = wgt
            rc_ref[g] = rc
            local = tn(b_ref[g], wgt).astype(BF16)
            first = tn(c_ref[g], rc).astype(BF16)
            for j in range(8):
                out_ref[h, block * 8 + j, :64, :] = local[:, j * HALF:(j + 1) * HALF]
                out_ref[h, block * 8 + j, 64:, :] = first[:, j * HALF:(j + 1) * HALF]
            if h == 0:
                to_eight(out_copy, own_copy, h, block)
            return carry

        lax.fori_loop(0, PAIRS, produce, 0)

    def send_totals(i, carry):
        tot_copy(lax.rem(me + i, n)).start()
        return carry

    lax.fori_loop(1, n, send_totals, 0)
    tots_ref[me] = tot_ref[...]

    dlog_ref[...] = jnp.zeros_like(dlog_ref)
    half = lax.broadcasted_iota(jnp.int32, (1, TOK), 1) < STATE
    left = jnp.where(half, 1.0, 0.0)
    left_b = left.astype(BF16)
    right_b = (1.0 - left).astype(BF16)
    bad = jnp.where(valid, 0.0, 1.0)

    def inside(g, carry):
        b, c = b_ref[g], c_ref[g]
        scores = nt(c, b)
        logs = pltpu.roll(logd_ref[...], lax.rem(HEADS - 16 * g, HEADS), 1)
        d_scores = jnp.zeros((TOK, TOK), F32)
        errs = []
        for q in range(8):
            lanes = pl.ds(pl.multiple_of(g * WIDE + q * 128, 128), 128)
            cot_p = cot_ref[:, lanes]
            disc_p = disc_ref[g, :, q * 128:(q + 1) * 128]
            stacked = jnp.concatenate([disc_p * left_b, disc_p * right_b], axis=0)
            d_mixed = nt(cot_p, stacked)
            mixed = []
            for k in range(2):
                head = 2 * q + k
                span = logs[:, head:head + 1] - logt_ref[pl.ds(g * 16 + head, 1), :]
                weights = jnp.exp(jnp.where(valid, span, -1e30))
                d_scores += d_mixed[:, k * TOK:(k + 1) * TOK] * weights
                mixed.append((weights * scores).astype(BF16))
            mixed = jnp.concatenate(mixed, axis=1)
            inner = nn(mixed, stacked)
            both = tn(mixed, cot_p)
            dd = both[:TOK] * left + both[TOK:] * (1.0 - left)
            dd_ref[g, :, q * 128:(q + 1) * 128] = dd.astype(BF16)
            errs.append(cot_p.astype(F32) * inner - disc_p.astype(F32) * dd)
        dlog_ref[...] += per_head(jnp.concatenate(errs, axis=1), gather_matrix(g))
        ds = d_scores.astype(BF16)
        dc_ref[g] = nn(ds, b)
        db_ref[g] = tn(ds, c)
        return carry

    lax.fori_loop(0, SPLIT, inside, 0)
    all_sent(out_copy, 0)
    all_blocks(out_copy, own_copy, 1)
    lax.fori_loop(SPLIT, GROUPS, inside, 0)
    loads[4].wait()
    loads[5].wait()
    pick_row = lax.broadcasted_iota(jnp.int32, (16, 16), 0)
    pick_col = lax.broadcasted_iota(jnp.int32, (16, 16), 1)
    pick = jnp.where(pick_col == pick_row + 2 * my_eighth, 1.0, 0.0).astype(BF16)
    picked = [nn(pick, init_ref[h]) for h in range(2)]
    turned = [picked[h][r:r + 1, i * 128:(i + 1) * 128] for h in range(2) for r in range(2) for i in range(32)]
    turned = jnp.transpose(jnp.concatenate(turned, axis=0)).astype(BF16)
    from_i = lax.broadcasted_iota(jnp.int32, (128, OWN), 0)
    to_p = lax.broadcasted_iota(jnp.int32, (128, OWN), 1)
    even = jnp.where(to_p == 2 * from_i, 1.0, 0.0).astype(BF16)
    odd = jnp.where(to_p == 2 * from_i + 1, 1.0, 0.0).astype(BF16)
    init_state = nn(turned[:64], even) + nn(turned[64:], odd)

    def total_in(i, carry):
        src = lax.rem(me + n - i, n)
        remote(tot_ref, tots_ref.at[src], s3.at[src], r3.at[src], (src, f)).wait_recv()
        return carry

    lax.fori_loop(1, n, total_in, 0)
    from_head = lax.broadcasted_iota(jnp.int32, (HEADS, HALF), 0)
    to_lane = lax.broadcasted_iota(jnp.int32, (HEADS, HALF), 1) // STATE
    for h in range(2):
        owned = jnp.where(from_head == to_lane + 64 * h + 2 * me, 1.0, 0.0).astype(BF16)
        lap_ref[h] = sum(nn(part_of, owned) for part_of in split3(tots_ref[:, 0, :]))

    def back_copy(h, to):
        return remote(back_ref.at[h, to], home_ref.at[h, me], s2.at[h, to], r2.at[h, me], (to, f))

    def own_back(h):
        return pltpu.make_async_copy(back_ref.at[h, me], home_ref.at[h, me], lsem.at[20 + h])

    for h in range(2):
        lanes = slice(h * HALF, (h + 1) * HALF)
        own_copy(h).wait()

        def arrive(i, carry):
            src = lax.rem(me + n - i, n)
            remote(out_ref.at[h, src], in_ref.at[h, src], s1.at[h, src], r1.at[h, src], (src, f)).wait_recv()
            return carry

        lax.fori_loop(1, n, arrive, 0)

        def laps(i, state):
            ahead, behind = state
            j = n - 1 - i
            back_ref[h, i, :64, :] = ahead.astype(BF16)
            back_ref[h, j, 64:, :] = behind.astype(BF16)
            ahead = lap_ref[h, pl.ds(i, 1), :] * ahead + in_ref[h, i, :64, :].astype(F32)
            behind = in_ref[h, j, 64:, :].astype(F32) + lap_ref[h, pl.ds(j, 1), :] * behind
            return ahead, behind

        lax.fori_loop(0, n, laps, (init_state[:, lanes], jnp.zeros((STATE, HALF), F32)))

        if h == 1:
            all_sent(back_copy, 0)
        all_blocks(back_copy, own_back, h)

    for h in range(2):
        own_back(h).wait()
    dstep_ref[...] = jnp.zeros_like(dstep_ref)

    def save(g):
        return pltpu.make_async_copy(disc_ref.at[g], gval_hbm.at[:, wide(g)], lsem.at[8 + g])

    def d_copies(h):
        copies = []
        for k in range(2):
            cols = slice(512 * k + 256 * h, 512 * k + 256 * h + 256)
            mine_d = dall.at[:128, cols]
            copies.append(link(50 + 4 * h + 2 * k, mine_d, dall.at[128:256, cols], far))
            copies.append(link(51 + 4 * h + 2 * k, mine_d, dall.at[256:384, cols], sib))
        return copies

    for h in range(2):

        def consume(i, carry):
            block = lax.rem(my_pair + PAIRS - i, PAIRS)
            g = 4 * h + block
            for j in range(8):
                src = block * 8 + j

                @pl.when(src != me)
                def _():
                    remote(back_ref.at[h, src], home_ref.at[h, src], s2.at[h, src], r2.at[h, src], (src, f)).wait_recv()

            got = jnp.concatenate([home_ref[h, block * 8 + j] for j in range(8)], axis=1)
            start, end = got[:64], got[64:]
            b, c = b_ref[g], c_ref[g]
            rc, wgt, disc = rc_ref[g], wgt_ref[g], disc_ref[g].astype(F32)
            carried = nn(c, start)
            d_wgt = nn(b, end)
            dc_ref[g] += nt(rc, start)
            db_ref[g] += nt(wgt, end)
            pull = wgt.astype(F32) * d_wgt
            mat = gather_matrix(g)
            err = rc.astype(F32) * carried - pull
            ends = jnp.sum(pull, axis=0, keepdims=True)
            ends += totx_ref[g, :1, :] * jnp.sum(start.astype(F32) * end.astype(F32), axis=0, keepdims=True)
            at_end = lax.broadcasted_iota(jnp.int32, (TOK, WIDE), 0) == TOK - 1
            err = err + jnp.where(at_end, ends, 0.0)
            dlog_ref[...] += per_head(err, mat)
            spread = nn(stack[TOK:2 * TOK], spread_matrix(g))
            d_disc = dd_ref[g].astype(F32) + spread * d_wgt
            val = val_ref[:, wide(g)].astype(F32)
            dstep_ref[...] += per_head(d_disc * val, mat)
            gval = skipx_ref[g, :1, :] * cot_ref[:, wide(g)].astype(F32) + step_ref[g] * d_disc
            disc_ref[g] = gval.astype(BF16)
            save(g).start()
            return carry

        lax.fori_loop(0, PAIRS, consume, 0)
        some = range(4 * h, 4 * h + 4)
        dall[:128, 256 * h:256 * h + 256] = jnp.concatenate([db_ref[g] for g in some], axis=1).astype(BF16)
        dall[:128, 512 + 256 * h:768 + 256 * h] = jnp.concatenate([dc_ref[g] for g in some], axis=1).astype(BF16)
        for one in d_copies(h):
            one.start()
    up_tri = jnp.where(col >= row, 1.0, 0.0).astype(BF16)
    d_inc = exact(up_tri, dlog_ref[...])
    d_step = dstep_ref[...] - rate_ref[...] * d_inc
    d_raw = d_step / (1.0 + jnp.exp(-raw))
    dall[:128, 1024:] = d_raw.astype(BF16)

    last_cols = pl.ds(1024, 128)
    d_last = dall.at[pl.ds(0, 128), last_cols]
    send_far = link(8, d_last, dall.at[pl.ds(128, 128), last_cols], far)
    send_far.start()
    send_sib = link(9, d_last, dall.at[pl.ds(256, 128), last_cols], sib)
    send_sib.start()
    gin_ref[:, pl.ds(mine, 1024)] = nt(dall[:128, :], w_ref[...]).astype(BF16)
    gin_ref[:, pl.ds(other, 1024)] = nt(dall[:128, :], wsib_ref[...]).astype(BF16)
    save_gin = pltpu.make_async_copy(gin_ref, gin_hbm.at[:, pl.ds(base, 2048)], lsem.at[7])
    save_gin.start()
    d_all = d_copies(0) + d_copies(1)
    for one in d_all[0::2]:
        one.wait_recv()
    send_far.wait_recv()
    send_dfwd = link(10, dall.at[pl.ds(128, 128), :], dall.at[pl.ds(384, 128), :], sib)
    send_dfwd.start()
    send_xo.wait_recv()
    send_fwd.wait_recv()
    for one in d_all[1::2]:
        one.wait_recv()
    send_sib.wait_recv()
    send_dfwd.wait_recv()

    def rows(at, count):
        return pl.ds(pl.multiple_of(at, count), count)

    def x_peer(x):
        return (me - my_x + x, f)

    def z_peer(z):
        return (me + 4 * (z - my_z), f)

    def row_peer(q):
        return (4 * q + my_x, f)

    def plane_peer(q):
        return (16 * (q // 4) + 4 * my_z + lax.rem(q, 4), f)

    def exchange(k, peer, mine_at, source, target, count=4):
        copies = []
        for step_to in range(1, count):
            to = lax.rem(mine_at + step_to, count)
            copies.append(remote(source(to), target(mine_at), ssem.at[k + to], rsem.at[k + mine_at], peer(to)))
        return copies

    def landed(k, peer, mine_at, source, target, count=4):
        for step_to in range(1, count):
            at = lax.rem(mine_at + step_to, count)
            remote(source(at), target(at), ssem.at[k + at], rsem.at[k + at], peer(at)).wait_recv()

    def product(at):
        part[rows(at, 128), :] = tn(xall[:, rows(at, 128)], dall[...]).astype(BF16)

    a_first = (12, x_peer, my_x, lambda x: part.at[rows(128 * x, 128), :], lambda x: ra1.at[x])
    b_first = (16, z_peer, my_z, lambda z: part.at[rows(512 + 128 * z, 128), :], lambda z: rb1.at[z])
    a_sent, b_sent = exchange(*a_first), exchange(*b_first)
    for k in range(3):
        product(128 * lax.rem(my_x + k + 1, 4))
        a_sent[k].start()
        product(512 + 128 * lax.rem(my_z + k + 1, 4))
        b_sent[k].start()
    product(128 * my_x)
    product(512 + 128 * my_z)
    ginfar_ref[:, pl.ds(mine, 1024)] = nt(dall[128:256, :], w_ref[...]).astype(BF16)
    ginfar_ref[:, pl.ds(other, 1024)] = nt(dall[128:256, :], wsib_ref[...]).astype(BF16)
    send_gin = link(11, ginfar_ref, gin_hbm.at[:, pl.ds(base, 2048)], far)
    send_gin.start()
    sent = a_sent + b_sent

    def summed(first, got, at, count=4):
        total = first.astype(F32)
        for step_to in range(1, count):
            total += got[lax.rem(at + step_to, count)].astype(F32)
        return total

    a_second = (20, row_peer, my_row, lambda q: a1.at[rows(16 * q, 16), :], lambda q: ra2.at[q], 8)
    b_second = (28, plane_peer, my_plane, lambda q: b1.at[rows(16 * q, 16), :], lambda q: rb2.at[q], 8)
    landed(*a_first)
    a1[...] = summed(part[rows(128 * my_x, 128), :], ra1, my_x).astype(BF16)
    a_sent = exchange(*a_second)
    for one in a_sent:
        one.start()
    landed(*b_first)
    b1[...] = summed(part[rows(512 + 128 * my_z, 128), :], rb1, my_z).astype(BF16)
    b_sent = exchange(*b_second)
    for one in b_sent:
        one.start()
    sent += a_sent + b_sent
    landed(*a_second)
    fa[...] = summed(a1[rows(16 * my_row, 16), :], ra2, my_row, 8).astype(BF16)
    a_third = (66, row_peer, my_row, lambda q: fa, lambda q: a128.at[rows(16 * q, 16), :], 8)
    a_sent = exchange(*a_third)
    for one in a_sent:
        one.start()
    landed(*b_second)
    fb[...] = summed(b1[rows(16 * my_plane, 16), :], rb2, my_plane, 8).astype(BF16)
    b_third = (74, plane_peer, my_plane, lambda q: fb, lambda q: b128.at[rows(16 * q, 16), :], 8)
    b_sent = exchange(*b_third)
    for one in b_sent:
        one.start()
    sent += a_sent + b_sent
    a128[rows(16 * my_row, 16), :] = fa[...]
    b128[rows(16 * my_plane, 16), :] = fb[...]
    a_last = (38, x_peer, my_x, lambda x: a128, lambda x: gw_hbm.at[rows(128 * x, 128), :])
    b_last = (42, z_peer, my_z, lambda z: b128, lambda z: gw_hbm.at[rows(512 + 128 * z, 128), :])
    landed(*a_third)
    a_sent = exchange(*a_last)
    for one in a_sent:
        one.start()
    landed(*b_third)
    b_sent = exchange(*b_last)
    for one in b_sent:
        one.start()
    sent += a_sent + b_sent
    keep = [
        pltpu.make_async_copy(a128, gw_hbm.at[rows(128 * my_x, 128), :], lsem.at[16]),
        pltpu.make_async_copy(b128, gw_hbm.at[rows(512 + 128 * my_z, 128), :], lsem.at[17]),
    ]
    for one in keep:
        one.start()

    def drain(i, carry):
        to = lax.rem(me + i, n)
        out_copy(1, to).wait_send()
        back_copy(1, to).wait_send()
        tot_copy(to).wait_send()
        return carry

    lax.fori_loop(1, n, drain, 0)
    for one in (send_x0, send_x1, send_w, send_xo, send_fwd, send_raw,
                send_far, send_sib, send_dfwd, send_gin):
        one.wait_send()
    for one in d_all + [bc_copy(u) for u in range(PAIRS)]:
        one.wait_send()
    send_gin.wait_recv()
    save_gin.wait()

    def saved(g, carry):
        save(g).wait()
        return carry

    lax.fori_loop(0, GROUPS, saved, 0)
    for one in keep:
        one.wait()
    landed(*a_last)
    landed(*b_last)
    for one in sent:
        one.wait_send()


def layer(x, w, val, cot, init, resets, bias, rate, skip):
    n = 32
    slab = (GROUPS, TOK, WIDE)
    hbm = pl.BlockSpec(memory_space=pl.ANY)
    vm = pltpu.VMEM
    dma = pltpu.SemaphoreType.DMA
    return pl.pallas_call(
        layer_kernel,
        out_shape=(
            jax.ShapeDtypeStruct((TOK, 4096), BF16),
            jax.ShapeDtypeStruct((TOK, GROUPS * WIDE), BF16),
            jax.ShapeDtypeStruct((1024, COLS), BF16),
        ),
        in_specs=[hbm] * 5 + [VMEM] * 4,
        out_specs=[hbm] * 3,
        scratch_shapes=[
            vm((TOK, 4096), BF16),
            vm((1024, COLS), BF16),
            vm((1024, COLS), BF16),
            vm((4 * TOK, 1024), BF16),
            vm((TOK, 1024), BF16),
            vm((TOK, COLS), F32),
            vm((TOK, COLS), F32),
            vm((TOK, HEADS), F32),
            vm((TOK, HEADS), F32),
            vm((PAIRS, TOK, 256), BF16),
            vm((PAIRS, TOK, 256), BF16),
            vm((GROUPS, TOK, STATE), BF16),
            vm((GROUPS, TOK, STATE), BF16),
            vm((TOK, GROUPS * WIDE), BF16),
            vm((TOK, GROUPS * WIDE), BF16),
            vm((2, 16, 4096), BF16),
            vm(slab, BF16),
            vm(slab, BF16),
            vm(slab, BF16),
            vm(slab, F32),
            vm((GROUPS, 8, WIDE), F32),
            vm((GROUPS, 8, WIDE), F32),
            vm(slab, BF16),
            vm((HEADS, TOK), F32),
            vm((TOK, HEADS), F32),
            vm((TOK, HEADS), F32),
            vm((TOK, HEADS), F32),
            vm((GROUPS, TOK, STATE), F32),
            vm((GROUPS, TOK, STATE), F32),
            vm((2, n, 128, HALF), BF16),
            vm((2, n, 128, HALF), BF16),
            vm((2, n, 128, HALF), BF16),
            vm((2, n, 128, HALF), BF16),
            vm((8, HEADS), F32),
            vm((n, 8, HEADS), F32),
            vm((2, n, HALF), F32),
            vm((4 * TOK, COLS), BF16),
            vm((TOK, 2048), BF16),
            vm((TOK, 2048), BF16),
            vm((1024, COLS), BF16),
            vm((4, 128, COLS), BF16),
            vm((4, 128, COLS), BF16),
            vm((128, COLS), BF16),
            vm((128, COLS), BF16),
            vm((8, 16, COLS), BF16),
            vm((8, 16, COLS), BF16),
            vm((16, COLS), BF16),
            vm((16, COLS), BF16),
            vm((128, COLS), BF16),
            vm((128, COLS), BF16),
            dma((82,)),
            dma((82,)),
            dma((22,)),
            dma((2, n)),
            dma((2, n)),
            dma((2, n)),
            dma((2, n)),
            dma((n,)),
            dma((n,)),
            pltpu.SemaphoreType.REGULAR,
            pltpu.SemaphoreType.REGULAR,
        ],
        compiler_params=pltpu.CompilerParams(
            collective_id=0, has_side_effects=True, vmem_limit_bytes=60 * 2**20
        ),
        name="layer",
    )(x, w, val, cot, init, resets, bias, rate, skip)


def finish_kernel(scale, gin, gval, gw, gin_out, gval_out, gw_out, narrow, full, gin_v, gval_v, sem_i, sem_o):
    def some(k):
        return pl.ds(128 * k, 128)

    def pick(k):
        return pl.ds(32 * k, 32)

    loads = [pltpu.make_async_copy(gw.at[some(k), :], narrow.at[some(k), :], sem_i.at[k]) for k in range(8)]
    stores = [pltpu.make_async_copy(full.at[some(k), :], gw_out.at[some(k), :], sem_o.at[k]) for k in range(8)]
    loads += [pltpu.make_async_copy(gval.at[pick(k), :], gval_v.at[pick(k), :], sem_i.at[8 + k]) for k in range(4)]
    stores += [pltpu.make_async_copy(gval_v.at[pick(k), :], gval_out.at[pick(k), :], sem_o.at[8 + k]) for k in range(4)]
    loads.append(pltpu.make_async_copy(gin, gin_v, sem_i.at[12]))
    stores.append(pltpu.make_async_copy(gin_v, gin_out, sem_o.at[12]))
    for one in loads:
        one.start()
    for k in range(13):
        loads[k].wait()
        if k < 8:
            full[some(k), :] = narrow[some(k), :].astype(F32) * scale
        stores[k].start()
    for one in stores:
        one.wait()


def finish(scale, gin, gval, gw):
    hbm = pl.BlockSpec(memory_space=pl.ANY)
    return pl.pallas_call(
        functools.partial(finish_kernel, scale),
        out_shape=(
            jax.ShapeDtypeStruct(gin.shape, BF16),
            jax.ShapeDtypeStruct(gval.shape, BF16),
            jax.ShapeDtypeStruct(gw.shape, F32),
        ),
        in_specs=[hbm] * 3,
        out_specs=[hbm] * 3,
        scratch_shapes=[
            pltpu.VMEM((1024, COLS), BF16),
            pltpu.VMEM((1024, COLS), F32),
            pltpu.VMEM((TOK, 4096), BF16),
            pltpu.VMEM((TOK, GROUPS * WIDE), BF16),
            pltpu.SemaphoreType.DMA((13,)),
            pltpu.SemaphoreType.DMA((13,)),
        ],
        compiler_params=pltpu.CompilerParams(vmem_limit_bytes=60 * 2**20),
        name="finish",
    )(gin, gval, gw)


def body(inputs, values, cotangent, weight, init_state, resets, dt_bias, decay_rate, skip):
    scale = 1.0 / math.sqrt(lax.axis_size("fsdp") * TOK * lax.axis_size("ctx"))
    gin, gval, gw = layer(inputs[0], weight, values[0], cotangent[0], init_state[0], resets,
                          dt_bias[None], decay_rate[None], skip[None])
    gin, gval, gw = finish(scale, gin, gval, gw)
    return (gin[None], gval[None], gw)


def solution(mesh):
    in_specs = (
        P("fsdp", "ctx", None),
        P("fsdp", "ctx", None),
        P("fsdp", "ctx", None),
        P("fsdp", None),
        P("fsdp", None, None),
        P("fsdp", "ctx"),
        P(),
        P(),
        P(),
    )
    out_specs = (P("fsdp", "ctx", None), P("fsdp", "ctx", None), P("fsdp", None))
    return jax.shard_map(body, mesh=mesh, in_specs=in_specs, out_specs=out_specs, check_vma=False)
```

time: 166 us -> 149 us (0.90)
  Pallas kernels: 157 us -> 148 us
  other arithmetic: 4.24 us -> 0 us
  local copies, waits for them, and re-layouts: 3.29 us -> 0 us
    pallas_call x1, Pallas kernels: 157 us -> 143 us  [layer(): pl.pallas_call(layer_kernel, out_shape=(jax.ShapeDtypeStruct((TOK, 4096),...]
    pallas_call x0 -> x1, Pallas kernels: none -> 5.34 us  [finish(): pl.pallas_call(functools.partial(finish_kernel, scale), out_shape=(jax.Sh...]
    mul x1 -> x0, other arithmetic: 4.24 us -> none  [body(): return (gin[None], gval[None], gw.astype(F32) * scale)]
    unnamed x6 -> x0, local copies, waits for them, and re-layouts: 3.29 us -> none
where the time goes in v3:
time: 149 us
  Pallas kernels  148 us (99%)
    pallas_call x1, Pallas kernels, layer(): pl.pallas_call(layer_kernel, out_shape=(jax.ShapeDtypeStruct((TOK, 4096),...  143 us
    pallas_call x1, Pallas kernels, finish(): pl.pallas_call(functools.partial(finish_kernel, scale), out_shape=(jax.Sh...  5.34 us

profile of v3, /device:TPU:0, one launch (start us, length us, event | category | flops | bytes accessed | tf_op | source)
XLA Modules:
  0.0 149.0 jit_solution(11868666221027301726)
XLA Ops:
  0.6 143.0 %layer.1 = (bf16[128,4096]{1,0:T(8,128)(2,1)}, bf16[128,8192]{1,0:T(8,128)(2,1)}, bf16[1024,1152]{1,0:T(8,128)(2,1)}) custom-call(bf16[128,4096]{1,0:T(8,128)(2,1)} %bitcast.11, bf16[1024,1152]{1,0:T(8,128)(2,1)} %w_hbm.1, bf16[128,8192]{1,0:T(8,128)(2,1)} %bitcast.9, bf16[128,8192]{1,0:T(8,128)(2,1)} %bitcast.10, bf16[128,4096]{1,0:T(8,128)(2,1)} %bitcast.12, ...), custom_call_target="tpu_custom_call" | custom-call | tf_op jit(solution)/shard_map/layer/pallas_call | solution.py:597
  143.7 5.3 %finish.1 = (bf16[128,4096]{1,0:T(8,128)(2,1)}, bf16[128,8192]{1,0:T(8,128)(2,1)}, f32[1024,1152]{1,0:T(8,128)}) custom-call(bf16[128,4096]{1,0:T(8,128)(2,1)} %get-tuple-element.9.gin, bf16[128,8192]{1,0:T(8,128)(2,1)} %get-tuple-element.10.gval, bf16[1024,1152]{1,0:T(8,128)(2,1)} %get-tuple-element.11.gw), custom_call_target="tpu_custom_call" | custom-call | tf_op jit(solution)/shard_map/finish/pallas_call | solution.py:702

commit v4 on v3

--- a/solution.py
+++ b/solution.py
@@ -20,7 +20,6 @@
 PAIRS = 4
 OWN = 256
 HALF = 128
-SPLIT = 4
 VMEM = pl.BlockSpec(memory_space=pltpu.VMEM)
 
 
@@ -92,7 +91,9 @@
                  b_ref, c_ref, val_ref, cot_ref, init_ref,
                  disc_ref, wgt_ref, rc_ref, step_ref, skipx_ref, totx_ref, dd_ref, logt_ref, logd_ref,
                  dlog_ref, dstep_ref, db_ref, dc_ref, out_ref, in_ref, back_ref, home_ref, tot_ref, tots_ref, lap_ref,
-                 dall, gin_ref, ginfar_ref, part, ra1, rb1, a1, b1, ra2, rb2, fa, fb, a128, b128,
+                 dall, gin_ref, ginfar_ref,
+                 part_0, part_1, ra1_0, ra1_1, rb1_0, rb1_1, a1_0, a1_1, b1_0, b1_1, ra2_0, ra2_1, rb2_0, rb2_1,
+                 fa_0, fa_1, fb_0, fb_1, a128_0, a128_1, b128_0, b128_1,
                  ssem, rsem, lsem, s1, r1, s2, r2, s3, r3, zsem, ysem):
     n = lax.axis_size("ctx")
     me, f = lax.axis_index("ctx"), lax.axis_index("fsdp")
@@ -260,8 +261,7 @@
             for j in range(8):
                 out_ref[h, block * 8 + j, :64, :] = local[:, j * HALF:(j + 1) * HALF]
                 out_ref[h, block * 8 + j, 64:, :] = first[:, j * HALF:(j + 1) * HALF]
-            if h == 0:
-                to_eight(out_copy, own_copy, h, block)
+            to_eight(out_copy, own_copy, h, block)
             return carry
 
         lax.fori_loop(0, PAIRS, produce, 0)
@@ -311,10 +311,7 @@
         db_ref[g] = tn(ds, c)
         return carry
 
-    lax.fori_loop(0, SPLIT, inside, 0)
-    all_sent(out_copy, 0)
-    all_blocks(out_copy, own_copy, 1)
-    lax.fori_loop(SPLIT, GROUPS, inside, 0)
+    lax.fori_loop(0, GROUPS, inside, 0)
     loads[4].wait()
     loads[5].wait()
     pick_row = lax.broadcasted_iota(jnp.int32, (16, 16), 0)
@@ -380,14 +377,145 @@
     def save(g):
         return pltpu.make_async_copy(disc_ref.at[g], gval_hbm.at[:, wide(g)], lsem.at[8 + g])
 
+    def rows(at, count):
+        return pl.ds(pl.multiple_of(at, count), count)
+
+    def x_peer(x):
+        return (me - my_x + x, f)
+
+    def z_peer(z):
+        return (me + 4 * (z - my_z), f)
+
+    def row_peer(q):
+        return (4 * q + my_x, f)
+
+    def plane_peer(q):
+        return (16 * (q // 4) + 4 * my_z + lax.rem(q, 4), f)
+
+    def exchange(k, peer, mine_at, source, target, count=4):
+        copies = []
+        for step_to in range(1, count):
+            to = lax.rem(mine_at + step_to, count)
+            copies.append(remote(source(to), target(mine_at), ssem.at[k + to], rsem.at[k + mine_at], peer(to)))
+        return copies
+
+    def landed(k, peer, mine_at, source, target, count=4):
+        for step_to in range(1, count):
+            at = lax.rem(mine_at + step_to, count)
+            remote(source(at), target(at), ssem.at[k + at], rsem.at[k + at], peer(at)).wait_recv()
+
+    def summed(first, got, at, count=4):
+        total = first.astype(F32)
+        for step_to in range(1, count):
+            total += got[lax.rem(at + step_to, count)].astype(F32)
+        return total
+
+    chunk_cols = (slice(0, 512), slice(512, 1152))
+    bufs = (
+        (part_0, ra1_0, rb1_0, a1_0, b1_0, ra2_0, rb2_0, fa_0, fb_0, a128_0, b128_0),
+        (part_1, ra1_1, rb1_1, a1_1, b1_1, ra2_1, rb2_1, fa_1, fb_1, a128_1, b128_1),
+    )
+    sent = []
+
+    def stages(c):
+        part, ra1, rb1, a1, b1, ra2, rb2, fa, fb, a128, b128 = bufs[c]
+        k = 100 * c
+        cols = chunk_cols[c]
+        return (
+            (k + 12, x_peer, my_x, lambda x: part.at[rows(128 * x, 128), :], lambda x: ra1.at[x]),
+            (k + 16, z_peer, my_z, lambda z: part.at[rows(512 + 128 * z, 128), :], lambda z: rb1.at[z]),
+            (k + 20, row_peer, my_row, lambda q: a1.at[rows(16 * q, 16), :], lambda q: ra2.at[q], 8),
+            (k + 28, plane_peer, my_plane, lambda q: b1.at[rows(16 * q, 16), :], lambda q: rb2.at[q], 8),
+            (k + 66, row_peer, my_row, lambda q: fa, lambda q: a128.at[rows(16 * q, 16), :], 8),
+            (k + 74, plane_peer, my_plane, lambda q: fb, lambda q: b128.at[rows(16 * q, 16), :], 8),
+            (k + 38, x_peer, my_x, lambda x: a128, lambda x: gw_hbm.at[rows(128 * x, 128), cols]),
+            (k + 42, z_peer, my_z, lambda z: b128, lambda z: gw_hbm.at[rows(512 + 128 * z, 128), cols]),
+        )
+
+    def go(stage):
+        copies = exchange(*stage)
+        for one in copies:
+            one.start()
+        sent.extend(copies)
+
     def d_copies(h):
-        copies = []
-        for k in range(2):
-            cols = slice(512 * k + 256 * h, 512 * k + 256 * h + 256)
-            mine_d = dall.at[:128, cols]
-            copies.append(link(50 + 4 * h + 2 * k, mine_d, dall.at[128:256, cols], far))
-            copies.append(link(51 + 4 * h + 2 * k, mine_d, dall.at[256:384, cols], sib))
-        return copies
+        cols = chunk_cols[h]
+        own_d, far_d = dall.at[:128, cols], dall.at[128:256, cols]
+        return (
+            link(50 + 3 * h, own_d, far_d, far),
+            link(51 + 3 * h, own_d, dall.at[256:384, cols], sib),
+            link(52 + 3 * h, far_d, dall.at[384:512, cols], sib),
+        )
+
+    def give_d(h):
+        for one in d_copies(h)[:2]:
+            one.start()
+
+    def first_stage(h):
+        to_far, to_sib, forward = d_copies(h)
+        to_far.wait_recv()
+        forward.start()
+        to_sib.wait_recv()
+        forward.wait_recv()
+        part, cols = bufs[h][0], chunk_cols[h]
+
+        def product(at):
+            part[rows(at, 128), :] = tn(xall[:, rows(at, 128)], dall[:, cols]).astype(BF16)
+
+        a_sent, b_sent = exchange(*stages(h)[0]), exchange(*stages(h)[1])
+        for k in range(3):
+            product(128 * lax.rem(my_x + k + 1, 4))
+            a_sent[k].start()
+            product(512 + 128 * lax.rem(my_z + k + 1, 4))
+            b_sent[k].start()
+        product(128 * my_x)
+        product(512 + 128 * my_z)
+        sent.extend(a_sent + b_sent)
+
+    def second_stage(c):
+        part, ra1, rb1, a1, b1 = bufs[c][:5]
+        stage = stages(c)
+        landed(*stage[0])
+        a1[...] = summed(part[rows(128 * my_x, 128), :], ra1, my_x).astype(BF16)
+        go(stage[2])
+        landed(*stage[1])
+        b1[...] = summed(part[rows(512 + 128 * my_z, 128), :], rb1, my_z).astype(BF16)
+        go(stage[3])
+
+    def third_stage(c):
+        a1, b1, ra2, rb2, fa, fb, a128, b128 = bufs[c][3:]
+        stage = stages(c)
+        landed(*stage[2])
+        fa[...] = summed(a1[rows(16 * my_row, 16), :], ra2, my_row, 8).astype(BF16)
+        go(stage[4])
+        landed(*stage[3])
+        fb[...] = summed(b1[rows(16 * my_plane, 16), :], rb2, my_plane, 8).astype(BF16)
+        go(stage[5])
+        a128[rows(16 * my_row, 16), :] = fa[...]
+        b128[rows(16 * my_plane, 16), :] = fb[...]
+
+    def keep(c):
+        a128, b128 = bufs[c][9:]
+        cols = chunk_cols[c]
+        return (
+            pltpu.make_async_copy(a128, gw_hbm.at[rows(128 * my_x, 128), cols], lsem.at[(16, 22)[c]]),
+            pltpu.make_async_copy(b128, gw_hbm.at[rows(512 + 128 * my_z, 128), cols], lsem.at[(17, 23)[c]]),
+        )
+
+    def last_stage(c):
+        stage = stages(c)
+        landed(*stage[4])
+        go(stage[6])
+        landed(*stage[5])
+        go(stage[7])
+        for one in keep(c):
+            one.start()
+
+    def input_product(at, target):
+        d = dall[at:at + 128, :]
+        d = jnp.concatenate([d[:, :256], d[:, 512:768], d[:, 256:512], d[:, 768:]], axis=1)
+        target[:, pl.ds(mine, 1024)] = nt(d, w_ref[...]).astype(BF16)
+        target[:, pl.ds(other, 1024)] = nt(d, wsib_ref[...]).astype(BF16)
 
     for h in range(2):
 
@@ -428,149 +556,45 @@
 
         lax.fori_loop(0, PAIRS, consume, 0)
         some = range(4 * h, 4 * h + 4)
-        dall[:128, 256 * h:256 * h + 256] = jnp.concatenate([db_ref[g] for g in some], axis=1).astype(BF16)
-        dall[:128, 512 + 256 * h:768 + 256 * h] = jnp.concatenate([dc_ref[g] for g in some], axis=1).astype(BF16)
-        for one in d_copies(h):
-            one.start()
+        at = 512 * h
+        dall[:128, at:at + 256] = jnp.concatenate([db_ref[g] for g in some], axis=1).astype(BF16)
+        dall[:128, at + 256:at + 512] = jnp.concatenate([dc_ref[g] for g in some], axis=1).astype(BF16)
+        if h == 0:
+            give_d(0)
     up_tri = jnp.where(col >= row, 1.0, 0.0).astype(BF16)
     d_inc = exact(up_tri, dlog_ref[...])
     d_step = dstep_ref[...] - rate_ref[...] * d_inc
-    d_raw = d_step / (1.0 + jnp.exp(-raw))
-    dall[:128, 1024:] = d_raw.astype(BF16)
-
-    last_cols = pl.ds(1024, 128)
-    d_last = dall.at[pl.ds(0, 128), last_cols]
-    send_far = link(8, d_last, dall.at[pl.ds(128, 128), last_cols], far)
-    send_far.start()
-    send_sib = link(9, d_last, dall.at[pl.ds(256, 128), last_cols], sib)
-    send_sib.start()
-    gin_ref[:, pl.ds(mine, 1024)] = nt(dall[:128, :], w_ref[...]).astype(BF16)
-    gin_ref[:, pl.ds(other, 1024)] = nt(dall[:128, :], wsib_ref[...]).astype(BF16)
+    dall[:128, 1024:] = (d_step / (1.0 + jnp.exp(-raw))).astype(BF16)
+    give_d(1)
+    send_xo.wait_recv()
+    send_fwd.wait_recv()
+    first_stage(0)
+    input_product(0, gin_ref)
     save_gin = pltpu.make_async_copy(gin_ref, gin_hbm.at[:, pl.ds(base, 2048)], lsem.at[7])
     save_gin.start()
-    d_all = d_copies(0) + d_copies(1)
-    for one in d_all[0::2]:
-        one.wait_recv()
-    send_far.wait_recv()
-    send_dfwd = link(10, dall.at[pl.ds(128, 128), :], dall.at[pl.ds(384, 128), :], sib)
-    send_dfwd.start()
-    send_xo.wait_recv()
-    send_fwd.wait_recv()
-    for one in d_all[1::2]:
-        one.wait_recv()
-    send_sib.wait_recv()
-    send_dfwd.wait_recv()
-
-    def rows(at, count):
-        return pl.ds(pl.multiple_of(at, count), count)
-
-    def x_peer(x):
-        return (me - my_x + x, f)
-
-    def z_peer(z):
-        return (me + 4 * (z - my_z), f)
-
-    def row_peer(q):
-        return (4 * q + my_x, f)
-
-    def plane_peer(q):
-        return (16 * (q // 4) + 4 * my_z + lax.rem(q, 4), f)
-
-    def exchange(k, peer, mine_at, source, target, count=4):
-        copies = []
-        for step_to in range(1, count):
-            to = lax.rem(mine_at + step_to, count)
-            copies.append(remote(source(to), target(mine_at), ssem.at[k + to], rsem.at[k + mine_at], peer(to)))
-        return copies
-
-    def landed(k, peer, mine_at, source, target, count=4):
-        for step_to in range(1, count):
-            at = lax.rem(mine_at + step_to, count)
-            remote(source(at), target(at), ssem.at[k + at], rsem.at[k + at], peer(at)).wait_recv()
-
-    def product(at):
-        part[rows(at, 128), :] = tn(xall[:, rows(at, 128)], dall[...]).astype(BF16)
-
-    a_first = (12, x_peer, my_x, lambda x: part.at[rows(128 * x, 128), :], lambda x: ra1.at[x])
-    b_first = (16, z_peer, my_z, lambda z: part.at[rows(512 + 128 * z, 128), :], lambda z: rb1.at[z])
-    a_sent, b_sent = exchange(*a_first), exchange(*b_first)
-    for k in range(3):
-        product(128 * lax.rem(my_x + k + 1, 4))
-        a_sent[k].start()
-        product(512 + 128 * lax.rem(my_z + k + 1, 4))
-        b_sent[k].start()
-    product(128 * my_x)
-    product(512 + 128 * my_z)
-    ginfar_ref[:, pl.ds(mine, 1024)] = nt(dall[128:256, :], w_ref[...]).astype(BF16)
-    ginfar_ref[:, pl.ds(other, 1024)] = nt(dall[128:256, :], wsib_ref[...]).astype(BF16)
+    first_stage(1)
+    second_stage(0)
+    input_product(128, ginfar_ref)
     send_gin = link(11, ginfar_ref, gin_hbm.at[:, pl.ds(base, 2048)], far)
+    third_stage(0)
+    second_stage(1)
+    third_stage(1)
+    last_stage(0)
     send_gin.start()
-    sent = a_sent + b_sent
-
-    def summed(first, got, at, count=4):
-        total = first.astype(F32)
-        for step_to in range(1, count):
-            total += got[lax.rem(at + step_to, count)].astype(F32)
-        return total
-
-    a_second = (20, row_peer, my_row, lambda q: a1.at[rows(16 * q, 16), :], lambda q: ra2.at[q], 8)
-    b_second = (28, plane_peer, my_plane, lambda q: b1.at[rows(16 * q, 16), :], lambda q: rb2.at[q], 8)
-    landed(*a_first)
-    a1[...] = summed(part[rows(128 * my_x, 128), :], ra1, my_x).astype(BF16)
-    a_sent = exchange(*a_second)
-    for one in a_sent:
-        one.start()
-    landed(*b_first)
-    b1[...] = summed(part[rows(512 + 128 * my_z, 128), :], rb1, my_z).astype(BF16)
-    b_sent = exchange(*b_second)
-    for one in b_sent:
-        one.start()
-    sent += a_sent + b_sent
-    landed(*a_second)
-    fa[...] = summed(a1[rows(16 * my_row, 16), :], ra2, my_row, 8).astype(BF16)
-    a_third = (66, row_peer, my_row, lambda q: fa, lambda q: a128.at[rows(16 * q, 16), :], 8)
-    a_sent = exchange(*a_third)
-    for one in a_sent:
-        one.start()
-    landed(*b_second)
-    fb[...] = summed(b1[rows(16 * my_plane, 16), :], rb2, my_plane, 8).astype(BF16)
-    b_third = (74, plane_peer, my_plane, lambda q: fb, lambda q: b128.at[rows(16 * q, 16), :], 8)
-    b_sent = exchange(*b_third)
-    for one in b_sent:
-        one.start()
-    sent += a_sent + b_sent
-    a128[rows(16 * my_row, 16), :] = fa[...]
-    b128[rows(16 * my_plane, 16), :] = fb[...]
-    a_last = (38, x_peer, my_x, lambda x: a128, lambda x: gw_hbm.at[rows(128 * x, 128), :])
-    b_last = (42, z_peer, my_z, lambda z: b128, lambda z: gw_hbm.at[rows(512 + 128 * z, 128), :])
-    landed(*a_third)
-    a_sent = exchange(*a_last)
-    for one in a_sent:
-        one.start()
-    landed(*b_third)
-    b_sent = exchange(*b_last)
-    for one in b_sent:
-        one.start()
-    sent += a_sent + b_sent
-    keep = [
-        pltpu.make_async_copy(a128, gw_hbm.at[rows(128 * my_x, 128), :], lsem.at[16]),
-        pltpu.make_async_copy(b128, gw_hbm.at[rows(512 + 128 * my_z, 128), :], lsem.at[17]),
-    ]
-    for one in keep:
-        one.start()
+    last_stage(1)
 
     def drain(i, carry):
         to = lax.rem(me + i, n)
+        out_copy(0, to).wait_send()
         out_copy(1, to).wait_send()
         back_copy(1, to).wait_send()
         tot_copy(to).wait_send()
         return carry
 
     lax.fori_loop(1, n, drain, 0)
-    for one in (send_x0, send_x1, send_w, send_xo, send_fwd, send_raw,
-                send_far, send_sib, send_dfwd, send_gin):
+    for one in (send_x0, send_x1, send_w, send_xo, send_fwd, send_raw, send_gin):
         one.wait_send()
-    for one in d_all + [bc_copy(u) for u in range(PAIRS)]:
+    for one in [*d_copies(0), *d_copies(1)] + [bc_copy(u) for u in range(PAIRS)]:
         one.wait_send()
     send_gin.wait_recv()
     save_gin.wait()
@@ -580,10 +604,11 @@
         return carry
 
     lax.fori_loop(0, GROUPS, saved, 0)
-    for one in keep:
-        one.wait()
-    landed(*a_last)
-    landed(*b_last)
+    for c in range(2):
+        for one in keep(c):
+            one.wait()
+        for stage in stages(c)[6:]:
+            landed(*stage)
     for one in sent:
         one.wait_send()
 
@@ -643,20 +668,12 @@
             vm((4 * TOK, COLS), BF16),
             vm((TOK, 2048), BF16),
             vm((TOK, 2048), BF16),
-            vm((1024, COLS), BF16),
-            vm((4, 128, COLS), BF16),
-            vm((4, 128, COLS), BF16),
-            vm((128, COLS), BF16),
-            vm((128, COLS), BF16),
-            vm((8, 16, COLS), BF16),
-            vm((8, 16, COLS), BF16),
-            vm((16, COLS), BF16),
-            vm((16, COLS), BF16),
-            vm((128, COLS), BF16),
-            vm((128, COLS), BF16),
-            dma((82,)),
-            dma((82,)),
-            dma((22,)),
+            *[vm(rows + (cols,), BF16)
+              for rows in ((1024,), (4, 128), (4, 128), (128,), (128,), (8, 16), (8, 16), (16,), (16,), (128,), (128,))
+              for cols in (512, 640)],
+            dma((182,)),
+            dma((182,)),
+            dma((24,)),
             dma((2, n)),
             dma((2, n)),
             dma((2, n)),
@@ -691,7 +708,8 @@
     for k in range(13):
         loads[k].wait()
         if k < 8:
-            full[some(k), :] = narrow[some(k), :].astype(F32) * scale
+            for to, at, wide in ((0, 0, 256), (256, 512, 256), (512, 256, 256), (768, 768, 384)):
+                full[some(k), to:to + wide] = narrow[some(k), at:at + wide].astype(F32) * scale
         stores[k].start()
     for one in stores:
         one.wait()

time: 149 us -> 141 us (0.946)
  Pallas kernels: 148 us -> 140 us
    pallas_call x1, Pallas kernels: 143 us -> 135 us  [layer(): pl.pallas_call(layer_kernel, out_shape=(jax.ShapeDtypeStruct((TOK, 4096),...]
where the time goes in v4:
time: 141 us
  Pallas kernels  140 us (99%)
    pallas_call x1, Pallas kernels, layer(): pl.pallas_call(layer_kernel, out_shape=(jax.ShapeDtypeStruct((TOK, 4096),...  135 us
    pallas_call x1, Pallas kernels, finish(): pl.pallas_call(functools.partial(finish_kernel, scale), out_shape=(jax.Sh...  5.34 us

profile of v4, /device:TPU:0, one launch (start us, length us, event | category | flops | bytes accessed | tf_op | source)
XLA Modules:
  0.0 141.1 jit_solution(853348246258480773)
XLA Ops:
  0.6 135.2 %layer.1 = (bf16[128,4096]{1,0:T(8,128)(2,1)}, bf16[128,8192]{1,0:T(8,128)(2,1)}, bf16[1024,1152]{1,0:T(8,128)(2,1)}) custom-call(bf16[128,4096]{1,0:T(8,128)(2,1)} %bitcast.11, bf16[1024,1152]{1,0:T(8,128)(2,1)} %w_hbm.1, bf16[128,8192]{1,0:T(8,128)(2,1)} %bitcast.9, bf16[128,8192]{1,0:T(8,128)(2,1)} %bitcast.10, bf16[128,4096]{1,0:T(8,128)(2,1)} %bitcast.12, ...), custom_call_target="tpu_custom_call" | custom-call | tf_op jit(solution)/shard_map/layer/pallas_call | solution.py:622
  135.8 5.3 %finish.1 = (bf16[128,4096]{1,0:T(8,128)(2,1)}, bf16[128,8192]{1,0:T(8,128)(2,1)}, f32[1024,1152]{1,0:T(8,128)}) custom-call(bf16[128,4096]{1,0:T(8,128)(2,1)} %get-tuple-element.9.gin, bf16[128,8192]{1,0:T(8,128)(2,1)} %get-tuple-element.10.gval, bf16[1024,1152]{1,0:T(8,128)(2,1)} %get-tuple-element.11.gw), custom_call_target="tpu_custom_call" | custom-call | tf_op jit(solution)/shard_map/finish/pallas_call | solution.py:720

commit v5 on v4

--- a/solution.py
+++ b/solution.py
@@ -205,24 +205,22 @@
     def tot_copy(to):
         return remote(tot_ref, tots_ref.at[me], s3.at[to], r3.at[me], (to, f))
 
-    def to_eight(copy, own, h, u):
-        for j in range(8):
-            to = u * 8 + lax.rem(my_eighth + j, 8)
-
-            @pl.when(to != me)
+    def spray(copy, own, h):
+        own(h).start()
+
+        def turn(t, carry):
+            to_x = lax.rem(my_x + t, 4)
+            to_z = lax.rem(my_z + t + t // 4, 4)
+            near = 16 * my_y + 4 * to_z + to_x
+            copy(h, 16 * (1 - my_y) + 4 * to_z + to_x).start()
+
+            @pl.when(t != 0)
             def _():
-                copy(h, to).start()
-
-            @pl.when(to == me)
-            def _():
-                own(h).start()
-
-    def all_blocks(copy, own, h):
-        def block(i, carry):
-            to_eight(copy, own, h, lax.rem(my_pair + i, PAIRS))
+                copy(h, near).start()
+
             return carry
 
-        lax.fori_loop(0, PAIRS, block, 0)
+        lax.fori_loop(0, 16, turn, 0)
 
     def all_sent(copy, h):
         def gone(i, carry):
@@ -261,10 +259,10 @@
             for j in range(8):
                 out_ref[h, block * 8 + j, :64, :] = local[:, j * HALF:(j + 1) * HALF]
                 out_ref[h, block * 8 + j, 64:, :] = first[:, j * HALF:(j + 1) * HALF]
-            to_eight(out_copy, own_copy, h, block)
             return carry
 
         lax.fori_loop(0, PAIRS, produce, 0)
+        spray(out_copy, own_copy, h)
 
     def send_totals(i, carry):
         tot_copy(lax.rem(me + i, n)).start()
@@ -366,9 +364,7 @@
 
         lax.fori_loop(0, n, laps, (init_state[:, lanes], jnp.zeros((STATE, HALF), F32)))
 
-        if h == 1:
-            all_sent(back_copy, 0)
-        all_blocks(back_copy, own_back, h)
+        spray(back_copy, own_back, h)
 
     for h in range(2):
         own_back(h).wait()
@@ -579,14 +575,15 @@
     third_stage(0)
     second_stage(1)
     third_stage(1)
+    send_gin.start()
     last_stage(0)
-    send_gin.start()
     last_stage(1)
 
     def drain(i, carry):
         to = lax.rem(me + i, n)
         out_copy(0, to).wait_send()
         out_copy(1, to).wait_send()
+        back_copy(0, to).wait_send()
         back_copy(1, to).wait_send()
         tot_copy(to).wait_send()
         return carry

time: 141 us -> 141 us (level)
  no operation moved by 1% of the time
where the time goes in v5:
time: 141 us; the launch traced here: 140 us
  Pallas kernels  140 us (99%)
    pallas_call x1, Pallas kernels, layer(): pl.pallas_call(layer_kernel, out_shape=(jax.ShapeDtypeStruct((TOK, 4096),...  134 us
    pallas_call x1, Pallas kernels, finish(): pl.pallas_call(functools.partial(finish_kernel, scale), out_shape=(jax.Sh...  5.34 us

profile of v5, /device:TPU:0, one launch (start us, length us, event | category | flops | bytes accessed | tf_op | source)
XLA Modules:
  0.0 140.5 jit_solution(6811098568362078203)
XLA Ops:
  0.6 134.5 %layer.1 = (bf16[128,4096]{1,0:T(8,128)(2,1)}, bf16[128,8192]{1,0:T(8,128)(2,1)}, bf16[1024,1152]{1,0:T(8,128)(2,1)}) custom-call(bf16[128,4096]{1,0:T(8,128)(2,1)} %bitcast.11, bf16[1024,1152]{1,0:T(8,128)(2,1)} %w_hbm.1, bf16[128,8192]{1,0:T(8,128)(2,1)} %bitcast.9, bf16[128,8192]{1,0:T(8,128)(2,1)} %bitcast.10, bf16[128,4096]{1,0:T(8,128)(2,1)} %bitcast.12, ...), custom_call_target="tpu_custom_call" | custom-call | tf_op jit(solution)/shard_map/layer/pallas_call | solution.py:619
  135.1 5.3 %finish.1 = (bf16[128,4096]{1,0:T(8,128)(2,1)}, bf16[128,8192]{1,0:T(8,128)(2,1)}, f32[1024,1152]{1,0:T(8,128)}) custom-call(bf16[128,4096]{1,0:T(8,128)(2,1)} %get-tuple-element.9.gin, bf16[128,8192]{1,0:T(8,128)(2,1)} %get-tuple-element.10.gval, bf16[1024,1152]{1,0:T(8,128)(2,1)} %get-tuple-element.11.gw), custom_call_target="tpu_custom_call" | custom-call | tf_op jit(solution)/shard_map/finish/pallas_call | solution.py:717

commit v6 on v5

--- a/solution.py
+++ b/solution.py
@@ -435,12 +435,19 @@
         sent.extend(copies)
 
     def d_copies(h):
-        cols = chunk_cols[h]
-        own_d, far_d = dall.at[:128, cols], dall.at[128:256, cols]
+        cols, whole = slice(512 * h, 512 * h + 512), chunk_cols[h]
+        own_d = dall.at[:128, cols]
         return (
-            link(50 + 3 * h, own_d, far_d, far),
+            link(50 + 3 * h, own_d, dall.at[128:256, cols], far),
             link(51 + 3 * h, own_d, dall.at[256:384, cols], sib),
-            link(52 + 3 * h, far_d, dall.at[384:512, cols], sib),
+            link(52 + 3 * h, dall.at[128:256, whole], dall.at[384:512, whole], sib),
+        )
+
+    def d_steps():
+        own_d = dall.at[:128, 1024:]
+        return (
+            link(56, own_d, dall.at[128:256, 1024:], far),
+            link(57, own_d, dall.at[256:384, 1024:], sib),
         )
 
     def give_d(h):
@@ -450,8 +457,12 @@
     def first_stage(h):
         to_far, to_sib, forward = d_copies(h)
         to_far.wait_recv()
+        if h == 1:
+            d_steps()[0].wait_recv()
         forward.start()
         to_sib.wait_recv()
+        if h == 1:
+            d_steps()[1].wait_recv()
         forward.wait_recv()
         part, cols = bufs[h][0], chunk_cols[h]
 
@@ -555,16 +566,16 @@
         at = 512 * h
         dall[:128, at:at + 256] = jnp.concatenate([db_ref[g] for g in some], axis=1).astype(BF16)
         dall[:128, at + 256:at + 512] = jnp.concatenate([dc_ref[g] for g in some], axis=1).astype(BF16)
-        if h == 0:
-            give_d(0)
+        give_d(h)
+    send_xo.wait_recv()
+    send_fwd.wait_recv()
+    first_stage(0)
     up_tri = jnp.where(col >= row, 1.0, 0.0).astype(BF16)
     d_inc = exact(up_tri, dlog_ref[...])
     d_step = dstep_ref[...] - rate_ref[...] * d_inc
     dall[:128, 1024:] = (d_step / (1.0 + jnp.exp(-raw))).astype(BF16)
-    give_d(1)
-    send_xo.wait_recv()
-    send_fwd.wait_recv()
-    first_stage(0)
+    for one in d_steps():
+        one.start()
     input_product(0, gin_ref)
     save_gin = pltpu.make_async_copy(gin_ref, gin_hbm.at[:, pl.ds(base, 2048)], lsem.at[7])
     save_gin.start()
@@ -591,7 +602,7 @@
     lax.fori_loop(1, n, drain, 0)
     for one in (send_x0, send_x1, send_w, send_xo, send_fwd, send_raw, send_gin):
         one.wait_send()
-    for one in [*d_copies(0), *d_copies(1)] + [bc_copy(u) for u in range(PAIRS)]:
+    for one in [*d_copies(0), *d_copies(1), *d_steps()] + [bc_copy(u) for u in range(PAIRS)]:
         one.wait_send()
     send_gin.wait_recv()
     save_gin.wait()

time: 141 us -> 141 us (level)
  no operation moved by 1% of the time
where the time goes in v6:
time: 141 us
  Pallas kernels  140 us (99%)
    pallas_call x1, Pallas kernels, layer(): pl.pallas_call(layer_kernel, out_shape=(jax.ShapeDtypeStruct((TOK, 4096),...  135 us
    pallas_call x1, Pallas kernels, finish(): pl.pallas_call(functools.partial(finish_kernel, scale), out_shape=(jax.Sh...  5.34 us

profile of v6, /device:TPU:0, one launch (start us, length us, event | category | flops | bytes accessed | tf_op | source)
XLA Modules:
  0.0 141.1 jit_solution(15164676429836694239)
XLA Ops:
  0.6 135.1 %layer.1 = (bf16[128,4096]{1,0:T(8,128)(2,1)}, bf16[128,8192]{1,0:T(8,128)(2,1)}, bf16[1024,1152]{1,0:T(8,128)(2,1)}) custom-call(bf16[128,4096]{1,0:T(8,128)(2,1)} %bitcast.11, bf16[1024,1152]{1,0:T(8,128)(2,1)} %w_hbm.1, bf16[128,8192]{1,0:T(8,128)(2,1)} %bitcast.9, bf16[128,8192]{1,0:T(8,128)(2,1)} %bitcast.10, bf16[128,4096]{1,0:T(8,128)(2,1)} %bitcast.12, ...), custom_call_target="tpu_custom_call" | custom-call | tf_op jit(solution)/shard_map/layer/pallas_call | solution.py:630
  135.8 5.3 %finish.1 = (bf16[128,4096]{1,0:T(8,128)(2,1)}, bf16[128,8192]{1,0:T(8,128)(2,1)}, f32[1024,1152]{1,0:T(8,128)}) custom-call(bf16[128,4096]{1,0:T(8,128)(2,1)} %get-tuple-element.9.gin, bf16[128,8192]{1,0:T(8,128)(2,1)} %get-tuple-element.10.gval, bf16[1024,1152]{1,0:T(8,128)(2,1)} %get-tuple-element.11.gw), custom_call_target="tpu_custom_call" | custom-call | tf_op jit(solution)/shard_map/finish/pallas_call | solution.py:728
